TPU v7x, 256 devices: a whole 4x4x8 slice. The times are simulated.
256 devices in a mesh: group: 4 (over y_hi, core), tp: 64 (over x, z, y_lo).
Axes of the slice: x: 4, y: 4 (y_hi: 2, y_lo: 2; y = y_hi * 2 + y_lo), z: 8, core: 2. Of those that a mesh axis runs over, the one named last changes fastest.
Arguments:
- tokens: bfloat16 [512, 8192], P(('group', 'tp')), may hold values from -7 to 7
- sequence_numbers: int32 [4, 128], P('group'), may hold values from 0 to 3, never falling along the last dimension, each value on 1 to 64 neighbouring positions
- query_projection_weight: bfloat16 [8192, 8192], P(None, 'tp'), may hold values from -1.1 to 1.1
- key_projection_weight: bfloat16 [8192, 1024], P(None, 'tp'), may hold values from -0.36 to 0.36
- value_projection_weight: bfloat16 [8192, 1024], P(None, 'tp'), may hold values from -0.0625 to 0.0625
- output_projection_weight: bfloat16 [8192, 8192], P('tp'), may hold values from -0.0625 to 0.0625
- attention_norm_gain: float32 [8192], replicated, may hold values from 0.1 to 1.9
- closing_norm_gain: float32 [8192], replicated, may hold values from 0.1 to 1.9
- projector: bfloat16 [8192, 3584], P('tp'), may hold values from -0.0625 to 0.0625
- student_hidden_rows: bfloat16 [512, 3584], P(('group', 'tp')), may hold values from -6 to 6
- student_norm_gain: float32 [3584], replicated, may hold values from 0.1 to 1.9
- adapter_down_map: bfloat16 [3584, 64], replicated, may hold values from -0.09375 to 0.09375
- adapter_up_map: bfloat16 [64, 3584], replicated, may hold values from -0.75 to 0.75
Outputs:
- token_loss: float32 [512], P(('group', 'tp'))
- grad_down: float32 [3584, 64], replicated
- grad_up: float32 [64, 3584], replicated
All inputs are finite; a program needn't handle non-finite values.
Results may differ from a plain program's by a relative error of at most 0.0045.
Values may be sent and summed in bfloat16 or wider, within the bound.
No kernel may reach another device: no remote copies, remote signals or barrier semaphores. Data moves between devices by JAX's collectives and lax.ppermute only.
A program may use at most 64 MiB of HBM per device.

v0:
```python
import jax
import jax.numpy as jnp
import numpy as np
from jax import lax
from jax.experimental import pallas as pl
from jax.experimental.pallas import tpu as pltpu
from jax.sharding import Mesh
from jax.sharding import PartitionSpec as P

D = 8192
H = 64
KV = 8
HD = 128
WIDTH = 3584
RANK = 64
TP = ("x", "z", "yl")
ALL = ("yh", "core", "x", "z", "yl")
WIDE = ("yh", "core", "x", "yl")

eps = 1e-06
VMEM_MB = 24
f32 = jnp.float32
bf16 = jnp.bfloat16
highest = lax.Precision.HIGHEST


def rms_norm(values, gain):
    mean_sq = jnp.mean(values * values, axis=-1, keepdims=True)
    return values * lax.rsqrt(mean_sq + eps) * gain


def exchange(blocks, axes):
    return lax.all_to_all(blocks, axes, split_axis=0, concat_axis=0, tiled=True)


def from_x(block, step):
    return lax.ppermute(block, "x", [((i + step) % 4, i) for i in range(4)])


def from_z(block, step):
    return lax.ppermute(block, "z", [((i + step) % 8, i) for i in range(8)])


def from_yl(block):
    return lax.ppermute(block, "yl", [(0, 1), (1, 0)])


def pick_rows():
    pick = np.zeros((2, 4, 8, 2, 2, 4, 8, 2, 4, 2, 2), np.float32)
    for x in range(4):
        for yl in range(2):
            for step, (sx, syl) in enumerate([(x, yl), ((x + 1) % 4, yl), (x, 1 - yl), ((x + 3) % 4, yl)]):
                for z in range(8):
                    for part in range(2):
                        for e in range(2):
                            pick[part, x, z, yl, e, sx, z, syl, step, part, e] = 1
    return pick.reshape(256, 1024)


def gained(part_ref, gain_ref, start):
    wide = part_ref[...].astype(f32)
    squares = jnp.sum(wide * wide, axis=1, keepdims=True)
    return (wide * gain_ref[:, pl.ds(start, D // 4)]).astype(bf16), squares


def own_quarter(colour_ref, mine_ref, gain_ref, kv_ref, served_ref):
    part, _ = gained(mine_ref, gain_ref, pl.multiple_of(colour_ref[0] * (D // 4), D // 4))
    served = lax.dot_general(kv_ref[...], part, (((1,), (1,)), ((), ())), preferred_element_type=f32).astype(bf16)
    for device in range(64):
        head = device // 8
        served_ref[device] = served[head * 16 : head * 16 + 16]


def attention(
    colour_ref,
    mine_ref,
    one_ref,
    two_ref,
    three_ref,
    gain_ref,
    served_ref,
    pick_ref,
    seg_ref,
    query_weight_ref,
    output_weight_ref,
    own_ref,
    send_one_ref,
    send_two_ref,
    send_three_ref,
    query_weight,
    output_weight,
    context_ref,
    sems,
):
    def start_of(step, size):
        return pl.multiple_of(lax.rem(colour_ref[0] + step, 4) * size, size)

    copies = []
    for step in range(4):
        rows = query_weight_ref.at[pl.ds(start_of(step, D // 4), D // 4)]
        copies.append(pltpu.make_async_copy(rows, query_weight.at[step], sems.at[step]))
    copies.append(pltpu.make_async_copy(output_weight_ref, output_weight, sems.at[4]))
    for copy in copies:
        copy.start()
    query = jnp.zeros((128, HD), f32)
    squares = jnp.zeros((128, 1), f32)
    for step, ref in enumerate((mine_ref, one_ref, two_ref, three_ref)):
        part, more = gained(ref, gain_ref, start_of(step, D // 4))
        squares = squares + more
        copies[step].wait()
        query = query + jnp.dot(part, query_weight[step], preferred_element_type=f32)
    scale = lax.rsqrt(squares / D + eps)
    query = (query * scale).astype(bf16)
    both = jnp.dot(pick_ref[...], served_ref[...], preferred_element_type=f32)
    scale = jnp.broadcast_to(scale, (128, 128)).T
    key_t = (both[:128] * scale).astype(bf16)
    value_t = (both[128:] * scale).astype(bf16)
    scores = jnp.dot(query, key_t, preferred_element_type=f32) * (1.0 / np.sqrt(np.float32(HD)))
    rows = lax.broadcasted_iota(jnp.int32, (128, 128), 0)
    columns = lax.broadcasted_iota(jnp.int32, (128, 128), 1)
    seg = jnp.broadcast_to(seg_ref[...].astype(f32), (128, 128))
    allowed = (rows >= columns) & (seg == seg.T)
    scores = jnp.where(allowed, scores, -1e30)
    weights = jnp.exp(scores - jnp.max(scores, axis=1, keepdims=True))
    weights = (weights / jnp.sum(weights, axis=1, keepdims=True)).astype(bf16)
    context_ref[...] = lax.dot_general(weights, value_t, (((1,), (1,)), ((), ())), preferred_element_type=f32)
    turned = jnp.concatenate([context_ref[pl.ds(start_of(step, 32), 32), :] for step in range(4)], axis=0).astype(bf16)
    copies[4].wait()
    for start in range(0, D, 1024):
        at = pl.ds(start, 1024)
        product = jnp.dot(turned, output_weight[:, at], preferred_element_type=f32)
        own_ref[:, at] = product[:32]
        send_one_ref[:, at] = product[32:64].astype(bf16)
        send_two_ref[:, at] = product[64:96].astype(bf16)
        send_three_ref[:, at] = product[96:].astype(bf16)


def project(
    colour_ref, columns_ref, raw_ref, gain_ref, projector_ref, own_ref, send_one_ref, send_two_ref, send_three_ref
):
    sums = []
    for x in range(4):
        for yl in range(2):
            part = jnp.zeros((32, HD), f32)
            for z in range(8):
                part = part + columns_ref[x * 16 + z * 2 + yl].astype(f32)
            sums.append(part)
    summed = jnp.concatenate([sums[2 * c] + sums[2 * ((c + 2) % 4) + 1] for c in range(4)], axis=0)
    resid = raw_ref[...].astype(f32) + summed
    squares = jnp.sum(resid * resid, axis=1, keepdims=True)
    high = squares.astype(bf16)
    low = (squares - high.astype(f32)).astype(bf16)
    lane = lax.broadcasted_iota(jnp.int32, (128, 128), 1)
    tail = jnp.where(lane == 0, high.astype(f32), jnp.where(lane == 1, low.astype(f32), 0.0)).astype(bf16)
    features = (resid * gain_ref[...]).astype(bf16)
    row = lax.broadcasted_iota(jnp.int32, (128, 128), 0)
    yl = (row >> 4) & 1
    x = (colour_ref[0] + (row >> 5) + 2 * yl) & 3
    token = 32 * x + 4 * ((row >> 1) & 7) + 2 * yl + (row & 1)
    order = jnp.where(lane == token, 1.0, 0.0).astype(bf16)
    features = jnp.dot(order, features, preferred_element_type=f32).astype(bf16)
    tail = jnp.dot(order, tail, preferred_element_type=f32)
    for start in range(0, WIDTH + 128, 512):
        at = pl.ds(start, min(512, WIDTH + 128 - start))
        product = tail if start == WIDTH else jnp.dot(features, projector_ref[:, at], preferred_element_type=f32)
        own_ref[:, at] = product[:32]
        send_one_ref[:, at] = product[32:64].astype(bf16)
        send_two_ref[:, at] = product[64:96].astype(bf16)
        send_three_ref[:, at] = product[96:].astype(bf16)


def same_colour():
    def index(x, z, yl):
        return x * 16 + z * 2 + yl

    return [
        [index(c, z, 0) for z in range(8)] + [index((c + 2) % 4, z, 1) for z in range(8)] for c in range(4)
    ]


def same_quarter():
    return [[c * 8 + quarter + 4 * half for c in range(32) for half in range(2)] for quarter in range(4)]


def spread(tokens_ref, out_ref):
    for colour in range(4):
        block = tokens_ref[:, colour * (D // 4) : (colour + 1) * (D // 4)]
        for z in range(8):
            for yl in range(2):
                out_ref[(colour + 2 * yl) % 4 * 16 + z * 2 + yl] = block


def vmem_call(kernel, ins, outs, scratch=(), hbm=0, flops=0):
    vmem = pl.BlockSpec(memory_space=pltpu.VMEM)
    return pl.pallas_call(
        kernel,
        out_shape=[jax.ShapeDtypeStruct(*out) for out in outs],
        in_specs=[pl.BlockSpec(memory_space=pltpu.SMEM)] + [vmem] * ins + [pl.BlockSpec(memory_space=pl.ANY)] * hbm,
        out_specs=[vmem] * len(outs),
        scratch_shapes=list(scratch),
        compiler_params=pltpu.CompilerParams(vmem_limit_bytes=VMEM_MB * 2**20),
        cost_estimate=pl.CostEstimate(flops=flops, bytes_accessed=2**22, transcendentals=0),
        name=kernel.__name__,
    )


def shards(
    tokens,
    sequence_numbers,
    query_projection_weight,
    key_projection_weight,
    value_projection_weight,
    output_projection_weight,
    attention_norm_gain,
    closing_norm_gain,
    projector,
    student_hidden_rows,
    student_norm_gain,
    adapter_down_map,
    adapter_up_map,
):
    tp_index = lax.axis_index(TP)
    colour = lax.rem(lax.axis_index("x") + 2 * lax.axis_index("yl"), 4)

    with jax.named_scope("tokens"):
        (by_colour,) = pl.pallas_call(
            spread,
            out_shape=[jax.ShapeDtypeStruct((64, 2, D // 4), bf16)],
            in_specs=[pl.BlockSpec(memory_space=pltpu.VMEM)],
            out_specs=[pl.BlockSpec(memory_space=pltpu.VMEM)],
            compiler_params=pltpu.CompilerParams(vmem_limit_bytes=VMEM_MB * 2**20),
        )(tokens)
        by_colour, key_columns, value_columns = lax.optimization_barrier(
            (by_colour, key_projection_weight, value_projection_weight)
        )
        mine = exchange(by_colour, TP).reshape(128, D // 4)
        parts = [mine, from_x(mine, 1), from_yl(mine), from_x(mine, 3)]
        at = lax.rem(tp_index, 16) * HD
        raw_cols = jnp.where(
            lax.axis_index("yl") == 0,
            lax.dynamic_slice_in_dim(parts[0], at, HD, 1),
            lax.dynamic_slice_in_dim(parts[2], at, HD, 1),
        )

    with jax.named_scope("kv_weights"):
        columns = jnp.stack([key_columns.T, value_columns.T]).reshape(2, 2, KV, D)

        def features(step):
            return lax.dynamic_slice_in_dim(columns, lax.rem(colour + step, 4) * (D // 4), D // 4, 3)

        kv = [features(step).reshape(32, D // 4) for step in range(4)]
        kv = [kv[0], from_x(kv[1], 3), from_yl(kv[2]), from_x(kv[3], 1)]
        kv = jnp.stack(kv).reshape(16, KV, D // 4).transpose(1, 0, 2).reshape(128, D // 4)

    with jax.named_scope("own_quarter"):
        gain = attention_norm_gain.reshape(1, D)
        where = colour.reshape(1)
        (served,) = vmem_call(own_quarter, 3, [((64, 16, 128), bf16)], flops=2**31)(where, mine, gain, kv)
        served = exchange(served, TP).reshape(1024, 128)

    with jax.named_scope("attention"):
        total, *sent = vmem_call(
            attention,
            8,
            [((32, D), f32)] + [((32, D), bf16)] * 3,
            scratch=[
                pltpu.VMEM((4, D // 4, HD), bf16),
                pltpu.VMEM((HD, D), bf16),
                pltpu.VMEM((128, HD), f32),
                pltpu.SemaphoreType.DMA((5,)),
            ],
            hbm=2,
            flops=2**31,
        )(
            where,
            *parts,
            gain,
            served,
            jnp.asarray(pick_rows(), bf16),
            sequence_numbers,
            query_projection_weight,
            output_projection_weight,
        )

    with jax.named_scope("output"):
        total = total + from_x(sent[0], 3).astype(f32) + from_yl(sent[1]).astype(f32) + from_x(sent[2], 1).astype(f32)
        columns = total.astype(bf16).reshape(32, 64, HD).transpose(1, 0, 2)
        columns = exchange(columns, TP)

    with jax.named_scope("target"):
        gain_cols = lax.dynamic_slice_in_dim(closing_norm_gain, tp_index * HD, HD, 0).reshape(1, HD)
        total, *sent = vmem_call(
            project, 4, [((32, WIDTH + 128), f32)] + [((32, WIDTH + 128), bf16)] * 3, flops=2**31
        )(where, columns, raw_cols, gain_cols, projector)
        total = total + from_x(sent[0], 3).astype(f32) + from_yl(sent[1]).astype(f32) + from_x(sent[2], 1).astype(f32)
        squares = total[:, WIDTH] + total[:, WIDTH + 1]
        high = squares.astype(bf16)
        low = (squares - high.astype(f32)).astype(bf16)
        tail = jnp.pad(jnp.stack([high, low], axis=1), ((0, 0), (0, 126)))
        rows_out = jnp.concatenate([total[:, :WIDTH].astype(bf16), tail], axis=1).reshape(16, 2, WIDTH + 128)
        rows_in = lax.all_to_all(rows_out, TP, split_axis=0, concat_axis=0, axis_index_groups=same_colour(), tiled=True)
        rows_in = jnp.sum(rows_in.astype(f32), axis=0)
        squares = rows_in[:, WIDTH] + rows_in[:, WIDTH + 1]
        target = rows_in[:, :WIDTH] * lax.rsqrt(squares / D + eps)[:, None]

    with jax.named_scope("student"):
        student = student_hidden_rows.astype(f32)
        student_normed = rms_norm(student, student_norm_gain).astype(bf16)
        lowrank = jnp.dot(student_normed, adapter_down_map, preferred_element_type=f32).astype(bf16)
        reached = student + jnp.dot(lowrank, adapter_up_map, preferred_element_type=f32)
        diff = reached - target
        token_loss = jnp.mean(diff * diff, axis=1)
        scaled = diff / jnp.sqrt(f32(512))
        back = lax.dot_general(
            scaled, adapter_up_map.astype(f32), (((1,), (1,)), ((), ())), precision=highest, preferred_element_type=f32
        )

    with jax.named_scope("columns"):

        def groups(v):
            return v.reshape(2, 28, 128).transpose(1, 0, 2)

        right = jnp.concatenate([back.astype(bf16), lowrank], axis=1)
        message = jnp.concatenate(
            [
                jnp.pad(jnp.concatenate([groups(student_normed), groups(scaled.astype(bf16))], axis=2), ((0, 4), (0, 0), (0, 0))),
                jnp.broadcast_to(right, (32, 2, 128)),
            ],
            axis=2,
        )
        message = jnp.broadcast_to(message[:, None], (32, 2, 2, 384)).reshape(64, 2, 384)
        message = lax.all_to_all(
            message, WIDE + ("z",), split_axis=0, concat_axis=0, axis_index_groups=same_quarter(), tiled=True
        ).reshape(128, 384)

        def product(left, right):
            return lax.dot_general(left, right, (((0,), (0,)), ((), ())), preferred_element_type=f32)

        down = product(message[:, 256:320], message[:, :128])
        up = product(message[:, 320:], message[:, 128:256])
        part = jnp.concatenate([down, up], axis=0).astype(bf16)
        one, two, three = (from_z(part, step).astype(f32) for step in (1, 2, 7))
        chunk = ((part.astype(f32) + two) + (one + three)).astype(bf16)

    with jax.named_scope("gradients"):
        whole = exchange(jnp.broadcast_to(chunk, (32, 128, 128)), WIDE)[:28].astype(f32)
        grad_down = whole[:, :64].transpose(0, 2, 1).reshape(WIDTH, RANK)
        grad_up = whole[:, 64:].transpose(1, 0, 2).reshape(RANK, WIDTH)
    return (token_loss, grad_down, grad_up)


def solution(mesh):
    fine = Mesh(np.asarray(mesh.devices).reshape(2, 2, 4, 8, 2), ALL)
    return jax.shard_map(
        shards,
        mesh=fine,
        in_specs=(
            P(ALL, None),
            P(("yh", "core"), None),
            P(None, TP),
            P(None, TP),
            P(None, TP),
            P(TP, None),
            P(),
            P(),
            P(TP, None),
            P(ALL, None),
            P(),
            P(),
            P(),
        ),
        out_specs=(P(ALL), P(), P()),
        check_vma=False,
    )
```

profile of v0, /device:TPU:1, one launch (start us, length us, event | category | flops | bytes accessed | tf_op | source)
XLA Modules:
  0.0 175.4 jit_solution(1015300236668363814)
XLA Ops:
  0.7 0.8 copy-done.1
  1.5 0.8 tokens.1
  2.3 13.5 %all-to-all-start = ((bf16[64,2,2048]{2,1,0:T(2,128)(2,1)}), bf16[64,2,2048]{2,1,0:T(2,128)(2,1)S(1)}, u32[]{:S(2)}, u32[]{:S(2)}) async-start(bf16[64,2,2048]{2,1,0:T(2,128)(2,1)} %tokens.1), calls=%async_computation | async-start | bytes 1048576 | tf_op jit(solution)/shard_map/tokens/all_to_all | solution.py:33
  15.9 1.1 collective-permute-start.4
  17.0 2.6 %collective-permute-start.5 = (bf16[32,2048]{1,0:T(8,128)(2,1)S(1)}, bf16[32,2048]{1,0:T(8,128)(2,1)S(1)}, u32[]{:S(2)}, u32[]{:S(2)}) collective-permute-start(bf16[32,2048]{1,0:T(8,128)(2,1)S(1)} %bitcast.57), channel_id=1, source_target_pairs={{16,0},{32,16},{48,32},{0,48},{17,1},{33,17},{49,33},{1,49},{18,2}... | collective-permute-start | bytes 393224 | tf_op jit(solution)/shard_map/kv_weights/ppermute | solution.py:37
  19.7 1.7 collective-permute-done.4
  21.4 1.7 collective-permute-done.5
  23.1 3.8 %collective-permute-done.3 = bf16[32,2048]{1,0:T(8,128)(2,1)S(1)} collective-permute-done((bf16[32,2048]{1,0:T(8,128)(2,1)S(1)}, bf16[32,2048]{1,0:T(8,128)(2,1)S(1)}, u32[]{:S(2)}, u32[]{:S(2)}) %collective-permute-start.3) | collective-permute-done | bytes 131104 | tf_op jit(solution)/shard_map/kv_weights/ppermute | solution.py:37
  27.0 0.3 copy.30
  27.3 4.1 %all-to-all-done = bf16[64,2,2048]{2,1,0:T(2,128)(2,1)S(1)} async-done(((bf16[64,2,2048]{2,1,0:T(2,128)(2,1)}), bf16[64,2,2048]{2,1,0:T(2,128)(2,1)S(1)}, u32[]{:S(2)}, u32[]{:S(2)}) %all-to-all-start) | async-done | bytes 524320 | tf_op jit(solution)/shard_map/tokens/all_to_all | solution.py:33
  31.4 0.2 reshape.79.mine_ref
  31.6 0.8 collective-permute-start.1
  32.4 2.4 %collective-permute-start = (bf16[128,2048]{1,0:T(8,128)(2,1)S(1)}, bf16[128,2048]{1,0:T(8,128)(2,1)S(1)}, u32[]{:S(2)}, u32[]{:S(2)}) collective-permute-start(bf16[128,2048]{1,0:T(8,128)(2,1)S(1)} %reshape.79.mine_ref), channel_id=1, source_target_pairs={{16,0},{32,16},{48,32},{0,48},{17,1},{33,17},{49,33},{1,49},{18,2}... | collective-permute-start | bytes 1572872 | tf_op jit(solution)/shard_map/tokens/ppermute | solution.py:37
  34.9 0.3 own_quarter.1
  35.2 17.5 %all_to_all.30 = bf16[64,16,128]{2,1,0:T(8,128)(2,1)S(1)} all-to-all(bf16[64,16,128]{2,1,0:T(8,128)(2,1)S(1)} %own_quarter.1), channel_id=1, replica_groups=mesh['yh'=2,'core'=2,'x'=4,'z'=8,'yl'=2] {'x','z','yl'}, dimensions={0} | all-to-all | bytes 524288 | tf_op jit(solution)/shard_map/own_quarter/all_to_all | solution.py:33
  52.8 3.4 %attention.1 = (f32[32,8192]{1,0:T(8,128)S(1)}, bf16[32,8192]{1,0:T(8,128)(2,1)S(1)}, bf16[32,8192]{1,0:T(8,128)(2,1)S(1)}, bf16[32,8192]{1,0:T(8,128)(2,1)S(1)}) custom-call(s32[1]{0:T(128)} %bitcast.colour_ref, bf16[128,2048]{1,0:T(8,128)(2,1)S(1)} %reshape.79.mine_ref, bf16[128,2048]{1,0:T(8,128)(2,1)S(1)} %collective-permute-done.one_ref, ...), custom_call_target="tpu_custom_call" | custom-call | flops 2147483648 | bytes 4194304 | tf_op jit(solution)/shard_map/attention/attention/pallas_call | solution.py:262
  56.2 0.6 collective-permute-start.6
  56.7 0.6 collective-permute-start.7
  57.4 2.3 %collective-permute-start.8 = (bf16[32,8192]{1,0:T(8,128)(2,1)S(1)}, bf16[32,8192]{1,0:T(8,128)(2,1)S(1)}, u32[]{:S(2)}, u32[]{:S(2)}) collective-permute-start(bf16[32,8192]{1,0:T(8,128)(2,1)S(1)} %get-tuple-element.20), channel_id=1, source_target_pairs={{16,0},{32,16},{48,32},{0,48},{17,1},{33,17},{49,33},{1,49},{18,2}... | collective-permute-start | bytes 1572872 | tf_op jit(solution)/shard_map/output/ppermute | solution.py:37
  59.6 7.1 %collective-permute-done.6 = bf16[32,8192]{1,0:T(8,128)(2,1)S(1)} collective-permute-done((bf16[32,8192]{1,0:T(8,128)(2,1)S(1)}, bf16[32,8192]{1,0:T(8,128)(2,1)S(1)}, u32[]{:S(2)}, u32[]{:S(2)}) %collective-permute-start.6) | collective-permute-done | bytes 524320 | tf_op jit(solution)/shard_map/output/ppermute | solution.py:37
  66.8 1.1 bitcast_bitcast_fusion
  67.9 9.0 %all-to-all-start.2 = ((bf16[64,32,128]{2,1,0:T(8,128)(2,1)}), bf16[64,32,128]{2,1,0:T(8,128)(2,1)S(1)}, u32[]{:S(2)}, u32[]{:S(2)}) async-start(bf16[64,32,128]{2,1,0:T(8,128)(2,1)} %bitcast_bitcast_fusion), calls=%async_computation.2 | async-start | bytes 1048576 | tf_op jit(solution)/shard_map/output/all_to_all | solution.py:33
  76.9 0.8 dynamic-slice_bitcast_fusion.gain_ref
  77.7 11.6 %all-to-all-done.2.columns_ref = bf16[64,32,128]{2,1,0:T(8,128)(2,1)S(1)} async-done(((bf16[64,32,128]{2,1,0:T(8,128)(2,1)}), bf16[64,32,128]{2,1,0:T(8,128)(2,1)S(1)}, u32[]{:S(2)}, u32[]{:S(2)}) %all-to-all-start.2) | async-done | bytes 524320 | tf_op jit(solution)/shard_map/output/all_to_all | solution.py:33
  89.3 0.6 project.1
  89.9 2.7 %collective-permute-start.11 = (bf16[32,3712]{1,0:T(8,128)(2,1)S(1)}, bf16[32,3712]{1,0:T(8,128)(2,1)S(1)}, u32[]{:S(2)}, u32[]{:S(2)}) collective-permute-start(bf16[32,3712]{1,0:T(8,128)(2,1)S(1)} %get-tuple-element.24), channel_id=1, source_target_pairs={{16,0},{32,16},{48,32},{0,48},{17,1},{33,17},{49,33},{1,49},{18,2}... | collective-permute-start | bytes 712712 | tf_op jit(solution)/shard_map/target/ppermute | solution.py:37
  92.8 2.7 %collective-permute-done.10 = bf16[32,3712]{1,0:T(8,128)(2,1)S(1)} collective-permute-done((bf16[32,3712]{1,0:T(8,128)(2,1)S(1)}, bf16[32,3712]{1,0:T(8,128)(2,1)S(1)}, u32[]{:S(2)}, u32[]{:S(2)}) %collective-permute-start.10) | collective-permute-done | bytes 237600 | tf_op jit(solution)/shard_map/target/ppermute | solution.py:45
  95.7 3.1 %collective-permute-done.9 = bf16[32,3712]{1,0:T(8,128)(2,1)S(1)} collective-permute-done((bf16[32,3712]{1,0:T(8,128)(2,1)S(1)}, bf16[32,3712]{1,0:T(8,128)(2,1)S(1)}, u32[]{:S(2)}, u32[]{:S(2)}) %collective-permute-start.9) | collective-permute-done | bytes 237600 | tf_op jit(solution)/shard_map/target/ppermute | solution.py:37
  99.5 0.8 reshape.90
  100.3 3.5 %all-to-all-start.3 = ((bf16[16,2,3712]{2,1,0:T(2,128)(2,1)}), bf16[16,2,3712]{2,1,0:T(2,128)(2,1)S(1)}, u32[]{:S(2)}, u32[]{:S(2)}) async-start(bf16[16,2,3712]{2,1,0:T(2,128)(2,1)} %reshape.90), calls=%async_computation.3 | async-start | bytes 475136 | tf_op jit(solution)/shard_map/target/all_to_all | solution.py:301
  104.0 0.2 convolution_convert_fusion.3
  104.2 9.7 %all-to-all-done.3 = bf16[16,2,3712]{2,1,0:T(2,128)(2,1)S(1)} async-done(((bf16[16,2,3712]{2,1,0:T(2,128)(2,1)}), bf16[16,2,3712]{2,1,0:T(2,128)(2,1)S(1)}, u32[]{:S(2)}, u32[]{:S(2)}) %all-to-all-start.3) | async-done | bytes 237600 | tf_op jit(solution)/shard_map/target/all_to_all | solution.py:301
  113.9 0.2 convert_reduce_fusion
  114.3 0.3 multiply_convert_fusion
  114.6 0.4 convolution_convert_fusion.2
  115.3 29.6 %all_to_all.31 = bf16[64,2,384]{2,1,0:T(2,128)(2,1)S(1)} all-to-all(bf16[64,2,384]{2,1,0:T(2,128)(2,1)S(1)} %bitcast.53), channel_id=1, replica_groups={{0,8,1,9,16,24,17,25,32,40,33,41,48,56,49,57,64,72,65,73,80,88,81,89,96..., dimensions={0} | all-to-all | bytes 196608 | tf_op jit(solution)/shard_map/columns/all_to_all | solution.py:332
  144.9 0.2 convolution_convert_fusion
  145.4 1.3 collective-permute-start.12
  146.7 1.5 collective-permute-start.14
  148.1 1.6 collective-permute-done.12
  149.8 1.0 collective-permute-done.14
  150.8 1.2 broadcast_in_dim.8
  152.0 5.4 %all-to-all-start.5 = ((bf16[32,128,128]{2,1,0:T(8,128)(2,1)}), bf16[32,128,128]{2,1,0:T(8,128)(2,1)S(1)}, u32[]{:S(2)}, u32[]{:S(2)}) async-start(bf16[32,128,128]{2,1,0:T(8,128)(2,1)} %broadcast_in_dim.8), calls=%async_computation.5 | async-start | bytes 2097152 | tf_op jit(solution)/shard_map/gradients/all_to_all | solution.py:33
  157.5 0.5 broadcast_multiply_fusion
  158.0 15.6 %all-to-all-done.5 = bf16[32,128,128]{2,1,0:T(8,128)(2,1)S(1)} async-done(((bf16[32,128,128]{2,1,0:T(8,128)(2,1)}), bf16[32,128,128]{2,1,0:T(8,128)(2,1)S(1)}, u32[]{:S(2)}, u32[]{:S(2)}) %all-to-all-start.5) | async-done | bytes 1048608 | tf_op jit(solution)/shard_map/gradients/all_to_all | solution.py:33
  173.6 0.2 slice_convert_fusion
  173.8 0.2 slice_bitcast_fusion
  174.0 1.4 copy_bitcast_fusion
  (66 shorter events, 2.2 us)
Async XLA Ops:
  0.6 113.7 %copy-start = (bf16[64,3584]{1,0:T(8,128)(2,1)S(1)}, bf16[64,3584]{1,0:T(8,128)(2,1)}, u32[]{:S(2)}) copy-start(bf16[64,3584]{1,0:T(8,128)(2,1)} %param.26) | copy-start | bytes 1376260
  0.6 0.8 copy-start.1
  1.5 14.4 %copy-start.8 = (bf16[8192,16]{0,1:T(8,128)(2,1)S(1)}, bf16[8192,16]{0,1:T(8,128)(2,1)}, u32[]{:S(2)}) copy-start(bf16[8192,16]{0,1:T(8,128)(2,1)} %param.17) | copy-start | bytes 786436
  1.5 14.4 %copy-start.9 = (bf16[8192,16]{0,1:T(8,128)(2,1)S(1)}, bf16[8192,16]{0,1:T(8,128)(2,1)}, u32[]{:S(2)}) copy-start(bf16[8192,16]{0,1:T(8,128)(2,1)} %param.18) | copy-start | bytes 786436
  2.3 29.1 %all-to-all-start = ((bf16[64,2,2048]{2,1,0:T(2,128)(2,1)}), bf16[64,2,2048]{2,1,0:T(2,128)(2,1)S(1)}, u32[]{:S(2)}, u32[]{:S(2)}) async-start(bf16[64,2,2048]{2,1,0:T(2,128)(2,1)} %tokens.1), calls=%async_computation | async-start | bytes 1048576 | tf_op jit(solution)/shard_map/tokens/all_to_all | solution.py:33
  15.9 19.0 %copy-start.5 = (f32[8192]{0:T(1024)S(1)}, f32[8192]{0:T(1024)}, u32[]{:S(2)}) copy-start(f32[8192]{0:T(1024)} %param.20) | copy-start | bytes 98308
  15.9 5.5 %collective-permute-start.4 = (bf16[32,2048]{1,0:T(8,128)(2,1)S(1)}, bf16[32,2048]{1,0:T(8,128)(2,1)S(1)}, u32[]{:S(2)}, u32[]{:S(2)}) collective-permute-start(bf16[32,2048]{1,0:T(8,128)(2,1)S(1)} %bitcast.59), channel_id=1, source_target_pairs={{0,1},{1,0},{2,3},{3,2},{4,5},{5,4},{6,7},{7,6},{8,9},{9,8},{10,11... | collective-permute-start | bytes 393224 | tf_op jit(solution)/shard_map/kv_weights/ppermute | solution.py:45
  17.0 6.1 %collective-permute-start.5 = (bf16[32,2048]{1,0:T(8,128)(2,1)S(1)}, bf16[32,2048]{1,0:T(8,128)(2,1)S(1)}, u32[]{:S(2)}, u32[]{:S(2)}) collective-permute-start(bf16[32,2048]{1,0:T(8,128)(2,1)S(1)} %bitcast.57), channel_id=1, source_target_pairs={{16,0},{32,16},{48,32},{0,48},{17,1},{33,17},{49,33},{1,49},{18,2}... | collective-permute-start | bytes 393224 | tf_op jit(solution)/shard_map/kv_weights/ppermute | solution.py:37
  19.6 7.3 %collective-permute-start.3 = (bf16[32,2048]{1,0:T(8,128)(2,1)S(1)}, bf16[32,2048]{1,0:T(8,128)(2,1)S(1)}, u32[]{:S(2)}, u32[]{:S(2)}) collective-permute-start(bf16[32,2048]{1,0:T(8,128)(2,1)S(1)} %bitcast.56), channel_id=1, source_target_pairs={{48,0},{0,16},{16,32},{32,48},{49,1},{1,17},{17,33},{33,49},{50,2}... | collective-permute-start | bytes 393224 | tf_op jit(solution)/shard_map/kv_weights/ppermute | solution.py:37
  31.6 21.2 %collective-permute-start.1 = (bf16[128,2048]{1,0:T(8,128)(2,1)S(1)}, bf16[128,2048]{1,0:T(8,128)(2,1)S(1)}, u32[]{:S(2)}, u32[]{:S(2)}) collective-permute-start(bf16[128,2048]{1,0:T(8,128)(2,1)S(1)} %reshape.79.mine_ref), channel_id=1, source_target_pairs={{0,1},{1,0},{2,3},{3,2},{4,5},{5,4},{6,7},{7,6},{8,9},{9,8},{10,11... | collective-permute-start | bytes 1572872 | tf_op jit(solution)/shard_map/tokens/ppermute | solution.py:45
  32.4 20.3 %collective-permute-start = (bf16[128,2048]{1,0:T(8,128)(2,1)S(1)}, bf16[128,2048]{1,0:T(8,128)(2,1)S(1)}, u32[]{:S(2)}, u32[]{:S(2)}) collective-permute-start(bf16[128,2048]{1,0:T(8,128)(2,1)S(1)} %reshape.79.mine_ref), channel_id=1, source_target_pairs={{16,0},{32,16},{48,32},{0,48},{17,1},{33,17},{49,33},{1,49},{18,2}... | collective-permute-start | bytes 1572872 | tf_op jit(solution)/shard_map/tokens/ppermute | solution.py:37
  34.9 17.9 %collective-permute-start.2 = (bf16[128,2048]{1,0:T(8,128)(2,1)S(1)}, bf16[128,2048]{1,0:T(8,128)(2,1)S(1)}, u32[]{:S(2)}, u32[]{:S(2)}) collective-permute-start(bf16[128,2048]{1,0:T(8,128)(2,1)S(1)} %reshape.79.mine_ref), channel_id=1, source_target_pairs={{48,0},{0,16},{16,32},{32,48},{49,1},{1,17},{17,33},{33,49},{50,2}... | collective-permute-start | bytes 1572872 | tf_op jit(solution)/shard_map/tokens/ppermute | solution.py:37
  34.9 17.9 %copy-start.2 = (bf16[8192,128]{1,0:T(8,128)(2,1)S(1)}, bf16[8192,128]{1,0:T(8,128)(2,1)}, u32[]{:S(2)}) copy-start(bf16[8192,128]{1,0:T(8,128)(2,1)} %query_weight_ref.1) | copy-start | bytes 6291460
  34.9 17.9 %copy-start.3 = (bf16[128,8192]{1,0:T(8,128)(2,1)S(1)}, bf16[128,8192]{1,0:T(8,128)(2,1)}, u32[]{:S(2)}) copy-start(bf16[128,8192]{1,0:T(8,128)(2,1)} %output_weight_ref.1) | copy-start | bytes 6291460
  34.9 17.9 %copy-start.6 = (s32[1,128]{1,0:T(1,128)S(1)}, s32[1,128]{1,0:T(1,128)}, u32[]{:S(2)}) copy-start(s32[1,128]{1,0:T(1,128)} %seg_ref.1) | copy-start | bytes 1540
  34.9 17.9 %copy-start.7 = (bf16[256,1024]{1,0:T(8,128)(2,1)S(1)}, bf16[256,1024]{1,0:T(8,128)(2,1)}, u32[]{:S(2)}) copy-start(bf16[256,1024]{1,0:T(8,128)(2,1)} %constant.64.clone.pick_ref) | copy-start | bytes 1572868
  56.2 10.6 %collective-permute-start.6 = (bf16[32,8192]{1,0:T(8,128)(2,1)S(1)}, bf16[32,8192]{1,0:T(8,128)(2,1)S(1)}, u32[]{:S(2)}, u32[]{:S(2)}) collective-permute-start(bf16[32,8192]{1,0:T(8,128)(2,1)S(1)} %get-tuple-element.18), channel_id=1, source_target_pairs={{48,0},{0,16},{16,32},{32,48},{49,1},{1,17},{17,33},{33,49},{50,2}... | collective-permute-start | bytes 1572872 | tf_op jit(solution)/shard_map/output/ppermute | solution.py:37
  56.7 10.0 %collective-permute-start.7 = (bf16[32,8192]{1,0:T(8,128)(2,1)S(1)}, bf16[32,8192]{1,0:T(8,128)(2,1)S(1)}, u32[]{:S(2)}, u32[]{:S(2)}) collective-permute-start(bf16[32,8192]{1,0:T(8,128)(2,1)S(1)} %get-tuple-element.19), channel_id=1, source_target_pairs={{0,1},{1,0},{2,3},{3,2},{4,5},{5,4},{6,7},{7,6},{8,9},{9,8},{10,11... | collective-permute-start | bytes 1572872 | tf_op jit(solution)/shard_map/output/ppermute | solution.py:45
  57.4 9.4 %collective-permute-start.8 = (bf16[32,8192]{1,0:T(8,128)(2,1)S(1)}, bf16[32,8192]{1,0:T(8,128)(2,1)S(1)}, u32[]{:S(2)}, u32[]{:S(2)}) collective-permute-start(bf16[32,8192]{1,0:T(8,128)(2,1)S(1)} %get-tuple-element.20), channel_id=1, source_target_pairs={{16,0},{32,16},{48,32},{0,48},{17,1},{33,17},{49,33},{1,49},{18,2}... | collective-permute-start | bytes 1572872 | tf_op jit(solution)/shard_map/output/ppermute | solution.py:37
  66.7 22.5 %copy-start.4 = (bf16[128,3584]{1,0:T(8,128)(2,1)S(1)}, bf16[128,3584]{1,0:T(8,128)(2,1)}, u32[]{:S(2)}) copy-start(bf16[128,3584]{1,0:T(8,128)(2,1)} %projector_ref.1) | copy-start | bytes 2752516
  67.9 21.4 %all-to-all-start.2 = ((bf16[64,32,128]{2,1,0:T(8,128)(2,1)}), bf16[64,32,128]{2,1,0:T(8,128)(2,1)S(1)}, u32[]{:S(2)}, u32[]{:S(2)}) async-start(bf16[64,32,128]{2,1,0:T(8,128)(2,1)} %bitcast_bitcast_fusion), calls=%async_computation.2 | async-start | bytes 1048576 | tf_op jit(solution)/shard_map/output/all_to_all | solution.py:33
  77.6 15.0 %copy-start.10 = (bf16[2,3584]{1,0:T(2,128)(2,1)S(1)}, bf16[2,3584]{1,0:T(2,128)(2,1)}, u32[]{:S(2)}) copy-start(bf16[2,3584]{1,0:T(2,128)(2,1)} %param.23) | copy-start | bytes 43012
  89.8 5.7 %collective-permute-start.10 = (bf16[32,3712]{1,0:T(8,128)(2,1)S(1)}, bf16[32,3712]{1,0:T(8,128)(2,1)S(1)}, u32[]{:S(2)}, u32[]{:S(2)}) collective-permute-start(bf16[32,3712]{1,0:T(8,128)(2,1)S(1)} %get-tuple-element.23), channel_id=1, source_target_pairs={{0,1},{1,0},{2,3},{3,2},{4,5},{5,4},{6,7},{7,6},{8,9},{9,8},{10,11... | collective-permute-start | bytes 712712 | tf_op jit(solution)/shard_map/target/ppermute | solution.py:45
  89.9 5.7 %collective-permute-start.11 = (bf16[32,3712]{1,0:T(8,128)(2,1)S(1)}, bf16[32,3712]{1,0:T(8,128)(2,1)S(1)}, u32[]{:S(2)}, u32[]{:S(2)}) collective-permute-start(bf16[32,3712]{1,0:T(8,128)(2,1)S(1)} %get-tuple-element.24), channel_id=1, source_target_pairs={{16,0},{32,16},{48,32},{0,48},{17,1},{33,17},{49,33},{1,49},{18,2}... | collective-permute-start | bytes 712712 | tf_op jit(solution)/shard_map/target/ppermute | solution.py:37
  92.6 6.2 %collective-permute-start.9 = (bf16[32,3712]{1,0:T(8,128)(2,1)S(1)}, bf16[32,3712]{1,0:T(8,128)(2,1)S(1)}, u32[]{:S(2)}, u32[]{:S(2)}) collective-permute-start(bf16[32,3712]{1,0:T(8,128)(2,1)S(1)} %get-tuple-element.22), channel_id=1, source_target_pairs={{48,0},{0,16},{16,32},{32,48},{49,1},{1,17},{17,33},{33,49},{50,2}... | collective-permute-start | bytes 712712 | tf_op jit(solution)/shard_map/target/ppermute | solution.py:37
  98.8 5.1 %copy-start.11 = (f32[3584]{0:T(1024)S(1)}, f32[3584]{0:T(1024)}, u32[]{:S(2)}) copy-start(f32[3584]{0:T(1024)} %param.24) | copy-start | bytes 43012
  98.8 5.2 %copy-start.12 = (bf16[3584,64]{0,1:T(8,128)(2,1)S(1)}, bf16[3584,64]{0,1:T(8,128)(2,1)}, u32[]{:S(2)}) copy-start(bf16[3584,64]{0,1:T(8,128)(2,1)} %param.25) | copy-start | bytes 1376260
  100.3 13.6 %all-to-all-start.3 = ((bf16[16,2,3712]{2,1,0:T(2,128)(2,1)}), bf16[16,2,3712]{2,1,0:T(2,128)(2,1)S(1)}, u32[]{:S(2)}, u32[]{:S(2)}) async-start(bf16[16,2,3712]{2,1,0:T(2,128)(2,1)} %reshape.90), calls=%async_computation.3 | async-start | bytes 475136 | tf_op jit(solution)/shard_map/target/all_to_all | solution.py:301
  145.4 4.4 %collective-permute-start.12 = (bf16[128,128]{1,0:T(8,128)(2,1)S(1)}, bf16[128,128]{1,0:T(8,128)(2,1)S(1)}, u32[]{:S(2)}, u32[]{:S(2)}) collective-permute-start(bf16[128,128]{1,0:T(8,128)(2,1)S(1)} %pad_maximum_fusion.2), channel_id=1, source_target_pairs={{4,0},{6,2},{8,4},{10,6},{12,8},{14,10},{0,12},{2,14},{5,1},{7,3},... | collective-permute-start | bytes 98312 | tf_op jit(solution)/shard_map/columns/ppermute | solution.py:41
  146.7 3.1 %collective-permute-start.13 = (bf16[128,128]{1,0:T(8,128)(2,1)S(1)}, bf16[128,128]{1,0:T(8,128)(2,1)S(1)}, u32[]{:S(2)}, u32[]{:S(2)}) collective-permute-start(bf16[128,128]{1,0:T(8,128)(2,1)S(1)} %pad_maximum_fusion.2), channel_id=1, source_target_pairs={{2,0},{4,2},{6,4},{8,6},{10,8},{12,10},{14,12},{0,14},{3,1},{5,3},... | collective-permute-start | bytes 98312 | tf_op jit(solution)/shard_map/columns/ppermute | solution.py:41
  146.7 4.1 %collective-permute-start.14 = (bf16[128,128]{1,0:T(8,128)(2,1)S(1)}, bf16[128,128]{1,0:T(8,128)(2,1)S(1)}, u32[]{:S(2)}, u32[]{:S(2)}) collective-permute-start(bf16[128,128]{1,0:T(8,128)(2,1)S(1)} %pad_maximum_fusion.2), channel_id=1, source_target_pairs={{14,0},{0,2},{2,4},{4,6},{6,8},{8,10},{10,12},{12,14},{15,1},{1,3}... | collective-permute-start | bytes 98312 | tf_op jit(solution)/shard_map/columns/ppermute | solution.py:41
  152.0 21.6 %all-to-all-start.5 = ((bf16[32,128,128]{2,1,0:T(8,128)(2,1)}), bf16[32,128,128]{2,1,0:T(8,128)(2,1)S(1)}, u32[]{:S(2)}, u32[]{:S(2)}) async-start(bf16[32,128,128]{2,1,0:T(8,128)(2,1)} %broadcast_in_dim.8), calls=%async_computation.5 | async-start | bytes 2097152 | tf_op jit(solution)/shard_map/gradients/all_to_all | solution.py:33
where the time goes:
time: 176 us; the launch traced here: 175 us
  waiting for transfers between devices  64 us (36%)
  starting transfers between devices  47.5 us (27%)
  blocking collectives  47.1 us (27%)
  local copies, waits for them, and re-layouts  6.34 us (4%)
  Pallas kernels  5.06 us (3%)
  other arithmetic  3.03 us (2%)
    all_to_all x3, waiting for transfers between devices, exchange(): return lax.all_to_all(blocks, axes, split_axis=0, concat_axis=0, tiled=True)  31.3 us
    all_to_all x1, blocking collectives, shards(): lax.all_to_all(message, WIDE + ('z',), split_axis=0, concat_axis=0, axis_...  29.6 us
    all_to_all x3, starting transfers between devices, exchange(): return lax.all_to_all(blocks, axes, split_axis=0, concat_axis=0, tiled=True)  27.9 us
    all_to_all x1, blocking collectives, exchange(): return lax.all_to_all(blocks, axes, split_axis=0, concat_axis=0, tiled=True)  17.5 us
    ppermute x8, waiting for transfers between devices, from_x(): return lax.ppermute(block, 'x', [((i + step) % 4, i) for i in range(4)])  15.9 us
    ppermute x8, starting transfers between devices, from_x(): return lax.ppermute(block, 'x', [((i + step) % 4, i) for i in range(4)])  10.6 us
    all_to_all x1, waiting for transfers between devices, shards(): lax.all_to_all(rows_out, TP, split_axis=0, concat_axis=0, axis_index_grou...  9.72 us
    ppermute x4, waiting for transfers between devices, from_yl(): return lax.ppermute(block, 'yl', [(0, 1), (1, 0)])  4.48 us
  transfers between devices with their start and end apart: 19, of which 13 were waited for; matrix products, arithmetic and copies ran while one was open for 1% of the time, Pallas kernels for 0%

commit v1 on v0

--- a/solution.py
+++ b/solution.py
@@ -87,28 +87,17 @@
     send_one_ref,
     send_two_ref,
     send_three_ref,
-    query_weight,
-    output_weight,
-    context_ref,
-    sems,
 ):
-    def start_of(step, size):
-        return pl.multiple_of(lax.rem(colour_ref[0] + step, 4) * size, size)
-
-    copies = []
-    for step in range(4):
-        rows = query_weight_ref.at[pl.ds(start_of(step, D // 4), D // 4)]
-        copies.append(pltpu.make_async_copy(rows, query_weight.at[step], sems.at[step]))
-    copies.append(pltpu.make_async_copy(output_weight_ref, output_weight, sems.at[4]))
-    for copy in copies:
-        copy.start()
+    def start_of(step):
+        return pl.multiple_of(lax.rem(colour_ref[0] + step, 4) * (D // 4), D // 4)
+
     query = jnp.zeros((128, HD), f32)
     squares = jnp.zeros((128, 1), f32)
     for step, ref in enumerate((mine_ref, one_ref, two_ref, three_ref)):
-        part, more = gained(ref, gain_ref, start_of(step, D // 4))
+        part, more = gained(ref, gain_ref, start_of(step))
         squares = squares + more
-        copies[step].wait()
-        query = query + jnp.dot(part, query_weight[step], preferred_element_type=f32)
+        rows = query_weight_ref[pl.ds(start_of(step), D // 4), :]
+        query = query + jnp.dot(part, rows, preferred_element_type=f32)
     scale = lax.rsqrt(squares / D + eps)
     query = (query * scale).astype(bf16)
     both = jnp.dot(pick_ref[...], served_ref[...], preferred_element_type=f32)
@@ -123,29 +112,23 @@
     scores = jnp.where(allowed, scores, -1e30)
     weights = jnp.exp(scores - jnp.max(scores, axis=1, keepdims=True))
     weights = (weights / jnp.sum(weights, axis=1, keepdims=True)).astype(bf16)
-    context_ref[...] = lax.dot_general(weights, value_t, (((1,), (1,)), ((), ())), preferred_element_type=f32)
-    turned = jnp.concatenate([context_ref[pl.ds(start_of(step, 32), 32), :] for step in range(4)], axis=0).astype(bf16)
-    copies[4].wait()
-    for start in range(0, D, 1024):
-        at = pl.ds(start, 1024)
-        product = jnp.dot(turned, output_weight[:, at], preferred_element_type=f32)
-        own_ref[:, at] = product[:32]
-        send_one_ref[:, at] = product[32:64].astype(bf16)
-        send_two_ref[:, at] = product[64:96].astype(bf16)
-        send_three_ref[:, at] = product[96:].astype(bf16)
+    context = lax.dot_general(weights, value_t, (((1,), (1,)), ((), ())), preferred_element_type=f32).astype(bf16)
+    refs = (own_ref, send_one_ref, send_two_ref, send_three_ref)
+    for step in range(4):
+        for z in range(8):
+            at = pl.multiple_of(start_of(step) + z * 256, 256)
+            product = jnp.dot(context, output_weight_ref[:, pl.ds(at, 256)], preferred_element_type=f32)
+            for yl in range(2):
+                ref = refs[(step + 2 * yl) % 4]
+                ref[yl * 8 + z] = product[:, yl * 128 : yl * 128 + 128].astype(ref.dtype)
 
 
 def project(
     colour_ref, columns_ref, raw_ref, gain_ref, projector_ref, own_ref, send_one_ref, send_two_ref, send_three_ref
 ):
-    sums = []
-    for x in range(4):
-        for yl in range(2):
-            part = jnp.zeros((32, HD), f32)
-            for z in range(8):
-                part = part + columns_ref[x * 16 + z * 2 + yl].astype(f32)
-            sums.append(part)
-    summed = jnp.concatenate([sums[2 * c] + sums[2 * ((c + 2) % 4) + 1] for c in range(4)], axis=0)
+    summed = jnp.zeros((128, HD), f32)
+    for device in range(16):
+        summed = summed + columns_ref[device].astype(f32)
     resid = raw_ref[...].astype(f32) + summed
     squares = jnp.sum(resid * resid, axis=1, keepdims=True)
     high = squares.astype(bf16)
@@ -190,14 +173,13 @@
                 out_ref[(colour + 2 * yl) % 4 * 16 + z * 2 + yl] = block
 
 
-def vmem_call(kernel, ins, outs, scratch=(), hbm=0, flops=0):
+def vmem_call(kernel, ins, outs, flops):
     vmem = pl.BlockSpec(memory_space=pltpu.VMEM)
     return pl.pallas_call(
         kernel,
         out_shape=[jax.ShapeDtypeStruct(*out) for out in outs],
-        in_specs=[pl.BlockSpec(memory_space=pltpu.SMEM)] + [vmem] * ins + [pl.BlockSpec(memory_space=pl.ANY)] * hbm,
+        in_specs=[pl.BlockSpec(memory_space=pltpu.SMEM)] + [vmem] * ins,
         out_specs=[vmem] * len(outs),
-        scratch_shapes=list(scratch),
         compiler_params=pltpu.CompilerParams(vmem_limit_bytes=VMEM_MB * 2**20),
         cost_estimate=pl.CostEstimate(flops=flops, bytes_accessed=2**22, transcendentals=0),
         name=kernel.__name__,
@@ -259,19 +241,8 @@
         served = exchange(served, TP).reshape(1024, 128)
 
     with jax.named_scope("attention"):
-        total, *sent = vmem_call(
-            attention,
-            8,
-            [((32, D), f32)] + [((32, D), bf16)] * 3,
-            scratch=[
-                pltpu.VMEM((4, D // 4, HD), bf16),
-                pltpu.VMEM((HD, D), bf16),
-                pltpu.VMEM((128, HD), f32),
-                pltpu.SemaphoreType.DMA((5,)),
-            ],
-            hbm=2,
-            flops=2**31,
-        )(
+        block = (16, 128, HD)
+        total, *sent = vmem_call(attention, 10, [(block, f32)] + [(block, bf16)] * 3, flops=2**31)(
             where,
             *parts,
             gain,
@@ -284,8 +255,9 @@
 
     with jax.named_scope("output"):
         total = total + from_x(sent[0], 3).astype(f32) + from_yl(sent[1]).astype(f32) + from_x(sent[2], 1).astype(f32)
-        columns = total.astype(bf16).reshape(32, 64, HD).transpose(1, 0, 2)
-        columns = exchange(columns, TP)
+        columns = lax.all_to_all(
+            total.astype(bf16), TP, split_axis=0, concat_axis=0, axis_index_groups=same_colour(), tiled=True
+        )
 
     with jax.named_scope("target"):
         gain_cols = lax.dynamic_slice_in_dim(closing_norm_gain, tp_index * HD, HD, 0).reshape(1, HD)

time: 176 us -> 173 us (0.983)
    all_to_all x0 -> x1, waiting for transfers between devices: none -> 11.9 us  [shards(): lax.all_to_all(total.astype(bf16), TP, split_axis=0, concat_axis=0, axis_...]
    all_to_all x3 -> x2, waiting for transfers between devices: 31.3 us -> 19.7 us  [exchange(): return lax.all_to_all(blocks, axes, split_axis=0, concat_axis=0, tiled=True)]
    all_to_all x3 -> x2, starting transfers between devices: 27.9 us -> 18.9 us  [exchange(): return lax.all_to_all(blocks, axes, split_axis=0, concat_axis=0, tiled=True)]
    all_to_all x0 -> x1, starting transfers between devices: none -> 6.67 us  [shards(): lax.all_to_all(total.astype(bf16), TP, split_axis=0, concat_axis=0, axis_...]
  transfers between devices with their start and end apart: 19 -> 19, of which waited for: 13 -> 12; matrix products, arithmetic and copies ran while one was open for 1% -> 1% of each run, Pallas kernels for 0% -> 0%
where the time goes in v1:
time: 173 us; the launch traced here: 172 us
  waiting for transfers between devices  64.3 us (37%)
  starting transfers between devices  46.6 us (27%)
  blocking collectives  45.9 us (27%)
  local copies, waits for them, and re-layouts  6.34 us (4%)
  Pallas kernels  3.83 us (2%)
  other arithmetic  3.02 us (2%)
    all_to_all x1, blocking collectives, shards(): lax.all_to_all(message, WIDE + ('z',), split_axis=0, concat_axis=0, axis_...  28.4 us
    all_to_all x2, waiting for transfers between devices, exchange(): return lax.all_to_all(blocks, axes, split_axis=0, concat_axis=0, tiled=True)  19.7 us
    all_to_all x2, starting transfers between devices, exchange(): return lax.all_to_all(blocks, axes, split_axis=0, concat_axis=0, tiled=True)  18.9 us
    all_to_all x1, blocking collectives, exchange(): return lax.all_to_all(blocks, axes, split_axis=0, concat_axis=0, tiled=True)  17.5 us
    ppermute x8, waiting for transfers between devices, from_x(): return lax.ppermute(block, 'x', [((i + step) % 4, i) for i in range(4)])  15.3 us
    all_to_all x1, waiting for transfers between devices, shards(): lax.all_to_all(total.astype(bf16), TP, split_axis=0, concat_axis=0, axis_...  11.9 us
    ppermute x8, starting transfers between devices, from_x(): return lax.ppermute(block, 'x', [((i + step) % 4, i) for i in range(4)])  10.3 us
    all_to_all x1, waiting for transfers between devices, shards(): lax.all_to_all(rows_out, TP, split_axis=0, concat_axis=0, axis_index_grou...  9.66 us
  transfers between devices with their start and end apart: 19, of which 12 were waited for; matrix products, arithmetic and copies ran while one was open for 1% of the time, Pallas kernels for 0%

profile of v1, /device:TPU:1, one launch (start us, length us, event | category | flops | bytes accessed | tf_op | source)
XLA Modules:
  0.0 172.4 jit_solution(11131700305686340321)
XLA Ops:
  0.7 0.8 copy-done.1
  1.5 0.8 tokens.1
  2.3 13.5 %all-to-all-start = ((bf16[64,2,2048]{2,1,0:T(2,128)(2,1)}), bf16[64,2,2048]{2,1,0:T(2,128)(2,1)S(1)}, u32[]{:S(2)}, u32[]{:S(2)}) async-start(bf16[64,2,2048]{2,1,0:T(2,128)(2,1)} %tokens.1), calls=%async_computation | async-start | bytes 1048576 | tf_op jit(solution)/shard_map/tokens/all_to_all | solution.py:33
  15.9 1.1 collective-permute-start.4
  17.0 2.6 %collective-permute-start.5 = (bf16[32,2048]{1,0:T(8,128)(2,1)S(1)}, bf16[32,2048]{1,0:T(8,128)(2,1)S(1)}, u32[]{:S(2)}, u32[]{:S(2)}) collective-permute-start(bf16[32,2048]{1,0:T(8,128)(2,1)S(1)} %bitcast.50), channel_id=1, source_target_pairs={{16,0},{32,16},{48,32},{0,48},{17,1},{33,17},{49,33},{1,49},{18,2}... | collective-permute-start | bytes 393224 | tf_op jit(solution)/shard_map/kv_weights/ppermute | solution.py:37
  19.7 1.7 %collective-permute-done.4 = bf16[32,2048]{1,0:T(8,128)(2,1)S(1)} collective-permute-done((bf16[32,2048]{1,0:T(8,128)(2,1)S(1)}, bf16[32,2048]{1,0:T(8,128)(2,1)S(1)}, u32[]{:S(2)}, u32[]{:S(2)}) %collective-permute-start.4) | collective-permute-done | bytes 131104 | tf_op jit(solution)/shard_map/kv_weights/ppermute | solution.py:45
  21.4 1.7 %collective-permute-done.5 = bf16[32,2048]{1,0:T(8,128)(2,1)S(1)} collective-permute-done((bf16[32,2048]{1,0:T(8,128)(2,1)S(1)}, bf16[32,2048]{1,0:T(8,128)(2,1)S(1)}, u32[]{:S(2)}, u32[]{:S(2)}) %collective-permute-start.5) | collective-permute-done | bytes 131104 | tf_op jit(solution)/shard_map/kv_weights/ppermute | solution.py:37
  23.1 3.8 %collective-permute-done.3 = bf16[32,2048]{1,0:T(8,128)(2,1)S(1)} collective-permute-done((bf16[32,2048]{1,0:T(8,128)(2,1)S(1)}, bf16[32,2048]{1,0:T(8,128)(2,1)S(1)}, u32[]{:S(2)}, u32[]{:S(2)}) %collective-permute-start.3) | collective-permute-done | bytes 131104 | tf_op jit(solution)/shard_map/kv_weights/ppermute | solution.py:37
  27.0 0.3 copy.28
  27.3 4.1 %all-to-all-done = bf16[64,2,2048]{2,1,0:T(2,128)(2,1)S(1)} async-done(((bf16[64,2,2048]{2,1,0:T(2,128)(2,1)}), bf16[64,2,2048]{2,1,0:T(2,128)(2,1)S(1)}, u32[]{:S(2)}, u32[]{:S(2)}) %all-to-all-start) | async-done | bytes 524320 | tf_op jit(solution)/shard_map/tokens/all_to_all | solution.py:33
  31.4 0.2 reshape.76.mine_ref
  31.6 0.8 collective-permute-start.1
  32.4 2.4 %collective-permute-start = (bf16[128,2048]{1,0:T(8,128)(2,1)S(1)}, bf16[128,2048]{1,0:T(8,128)(2,1)S(1)}, u32[]{:S(2)}, u32[]{:S(2)}) collective-permute-start(bf16[128,2048]{1,0:T(8,128)(2,1)S(1)} %reshape.76.mine_ref), channel_id=1, source_target_pairs={{16,0},{32,16},{48,32},{0,48},{17,1},{33,17},{49,33},{1,49},{18,2}... | collective-permute-start | bytes 1572872 | tf_op jit(solution)/shard_map/tokens/ppermute | solution.py:37
  34.9 0.3 own_quarter.1
  35.2 17.5 %all_to_all.30 = bf16[64,16,128]{2,1,0:T(8,128)(2,1)S(1)} all-to-all(bf16[64,16,128]{2,1,0:T(8,128)(2,1)S(1)} %own_quarter.1), channel_id=1, replica_groups=mesh['yh'=2,'core'=2,'x'=4,'z'=8,'yl'=2] {'x','z','yl'}, dimensions={0} | all-to-all | bytes 524288 | tf_op jit(solution)/shard_map/own_quarter/all_to_all | solution.py:33
  52.8 2.1 %attention.1 = (f32[16,128,128]{2,1,0:T(8,128)S(1)}, bf16[16,128,128]{2,1,0:T(8,128)(2,1)S(1)}, bf16[16,128,128]{2,1,0:T(8,128)(2,1)S(1)}, bf16[16,128,128]{2,1,0:T(8,128)(2,1)S(1)}) custom-call(s32[1]{0:T(128)} %bitcast.colour_ref, bf16[128,2048]{1,0:T(8,128)(2,1)S(1)} %reshape.76.mine_ref, bf16[128,2048]{1,0:T(8,128)(2,1)S(1)} %collective-permute-done.one_ref, ...), custom_call_target="tpu_custom_call" | custom-call | flops 2147483648 | bytes 4194304 | tf_op jit(solution)/shard_map/attention/attention/pallas_call | solution.py:245
  54.9 0.6 collective-permute-start.6
  55.5 0.6 collective-permute-start.7
  56.1 2.3 %collective-permute-start.8 = (bf16[16,128,128]{2,1,0:T(8,128)(2,1)S(1)}, bf16[16,128,128]{2,1,0:T(8,128)(2,1)S(1)}, u32[]{:S(2)}, u32[]{:S(2)}) collective-permute-start(bf16[16,128,128]{2,1,0:T(8,128)(2,1)S(1)} %get-tuple-element.20), channel_id=1, source_target_pairs={{16,0},{32,16},{48,32},{0,48},{17,1},{33,17},{49,33},{1,49},{18,2}... | collective-permute-start | bytes 1572872 | tf_op jit(solution)/shard_map/output/ppermute | solution.py:37
  58.4 7.1 %collective-permute-done.6 = bf16[16,128,128]{2,1,0:T(8,128)(2,1)S(1)} collective-permute-done((bf16[16,128,128]{2,1,0:T(8,128)(2,1)S(1)}, bf16[16,128,128]{2,1,0:T(8,128)(2,1)S(1)}, u32[]{:S(2)}, u32[]{:S(2)}) %collective-permute-start.6) | collective-permute-done | bytes 524320 | tf_op jit(solution)/shard_map/output/ppermute | solution.py:37
  65.5 1.1 add_convert_fusion
  66.6 6.7 %all-to-all-start.2 = ((bf16[16,128,128]{2,1,0:T(8,128)(2,1)}), bf16[16,128,128]{2,1,0:T(8,128)(2,1)S(1)}, u32[]{:S(2)}, u32[]{:S(2)}) async-start(bf16[16,128,128]{2,1,0:T(8,128)(2,1)} %add_convert_fusion), calls=%async_computation.2 | async-start | bytes 1048576 | tf_op jit(solution)/shard_map/output/all_to_all | solution.py:258
  73.3 0.8 dynamic-slice_bitcast_fusion.gain_ref
  74.1 11.9 %all-to-all-done.2.columns_ref = bf16[16,128,128]{2,1,0:T(8,128)(2,1)S(1)} async-done(((bf16[16,128,128]{2,1,0:T(8,128)(2,1)}), bf16[16,128,128]{2,1,0:T(8,128)(2,1)S(1)}, u32[]{:S(2)}, u32[]{:S(2)}) %all-to-all-start.2) | async-done | bytes 524320 | tf_op jit(solution)/shard_map/output/all_to_all | solution.py:258
  86.0 0.6 project.1
  86.7 2.4 %collective-permute-start.11 = (bf16[32,3712]{1,0:T(8,128)(2,1)S(1)}, bf16[32,3712]{1,0:T(8,128)(2,1)S(1)}, u32[]{:S(2)}, u32[]{:S(2)}) collective-permute-start(bf16[32,3712]{1,0:T(8,128)(2,1)S(1)} %get-tuple-element.24), channel_id=1, source_target_pairs={{16,0},{32,16},{48,32},{0,48},{17,1},{33,17},{49,33},{1,49},{18,2}... | collective-permute-start | bytes 712712 | tf_op jit(solution)/shard_map/target/ppermute | solution.py:37
  89.2 3.3 %collective-permute-done.10 = bf16[32,3712]{1,0:T(8,128)(2,1)S(1)} collective-permute-done((bf16[32,3712]{1,0:T(8,128)(2,1)S(1)}, bf16[32,3712]{1,0:T(8,128)(2,1)S(1)}, u32[]{:S(2)}, u32[]{:S(2)}) %collective-permute-start.10) | collective-permute-done | bytes 237600 | tf_op jit(solution)/shard_map/target/ppermute | solution.py:45
  92.5 2.7 %collective-permute-done.9 = bf16[32,3712]{1,0:T(8,128)(2,1)S(1)} collective-permute-done((bf16[32,3712]{1,0:T(8,128)(2,1)S(1)}, bf16[32,3712]{1,0:T(8,128)(2,1)S(1)}, u32[]{:S(2)}, u32[]{:S(2)}) %collective-permute-start.9) | collective-permute-done | bytes 237600 | tf_op jit(solution)/shard_map/target/ppermute | solution.py:37
  96.0 0.8 reshape.86
  96.8 5.2 %all-to-all-start.3 = ((bf16[16,2,3712]{2,1,0:T(2,128)(2,1)}), bf16[16,2,3712]{2,1,0:T(2,128)(2,1)S(1)}, u32[]{:S(2)}, u32[]{:S(2)}) async-start(bf16[16,2,3712]{2,1,0:T(2,128)(2,1)} %reshape.86), calls=%async_computation.3 | async-start | bytes 475136 | tf_op jit(solution)/shard_map/target/all_to_all | solution.py:273
  102.2 0.2 convolution_convert_fusion.3
  102.4 9.7 %all-to-all-done.3 = bf16[16,2,3712]{2,1,0:T(2,128)(2,1)S(1)} async-done(((bf16[16,2,3712]{2,1,0:T(2,128)(2,1)}), bf16[16,2,3712]{2,1,0:T(2,128)(2,1)S(1)}, u32[]{:S(2)}, u32[]{:S(2)}) %all-to-all-start.3) | async-done | bytes 237600 | tf_op jit(solution)/shard_map/target/all_to_all | solution.py:273
  112.0 0.2 convert_reduce_fusion
  112.4 0.3 multiply_convert_fusion
  112.7 0.4 convolution_convert_fusion.2
  113.4 28.4 %all_to_all.31 = bf16[64,2,384]{2,1,0:T(2,128)(2,1)S(1)} all-to-all(bf16[64,2,384]{2,1,0:T(2,128)(2,1)S(1)} %bitcast.46), channel_id=1, replica_groups={{0,8,1,9,16,24,17,25,32,40,33,41,48,56,49,57,64,72,65,73,80,88,81,89,96..., dimensions={0} | all-to-all | bytes 196608 | tf_op jit(solution)/shard_map/columns/all_to_all | solution.py:304
  141.9 0.2 convolution_convert_fusion
  142.4 1.3 collective-permute-start.12
  143.7 1.5 collective-permute-start.14
  145.1 1.6 collective-permute-done.12
  146.8 1.0 collective-permute-done.14
  147.8 1.2 broadcast_in_dim.8
  149.0 5.4 %all-to-all-start.5 = ((bf16[32,128,128]{2,1,0:T(8,128)(2,1)}), bf16[32,128,128]{2,1,0:T(8,128)(2,1)S(1)}, u32[]{:S(2)}, u32[]{:S(2)}) async-start(bf16[32,128,128]{2,1,0:T(8,128)(2,1)} %broadcast_in_dim.8), calls=%async_computation.5 | async-start | bytes 2097152 | tf_op jit(solution)/shard_map/gradients/all_to_all | solution.py:33
  154.5 0.5 broadcast_multiply_fusion
  155.0 15.6 %all-to-all-done.5 = bf16[32,128,128]{2,1,0:T(8,128)(2,1)S(1)} async-done(((bf16[32,128,128]{2,1,0:T(8,128)(2,1)}), bf16[32,128,128]{2,1,0:T(8,128)(2,1)S(1)}, u32[]{:S(2)}, u32[]{:S(2)}) %all-to-all-start.5) | async-done | bytes 1048608 | tf_op jit(solution)/shard_map/gradients/all_to_all | solution.py:33
  170.6 0.2 slice_convert_fusion
  170.8 0.2 slice_bitcast_fusion
  171.0 1.4 copy_bitcast_fusion
  (66 shorter events, 2.0 us)
Async XLA Ops:
  0.6 111.8 %copy-start = (bf16[64,3584]{1,0:T(8,128)(2,1)S(1)}, bf16[64,3584]{1,0:T(8,128)(2,1)}, u32[]{:S(2)}) copy-start(bf16[64,3584]{1,0:T(8,128)(2,1)} %param.26) | copy-start | bytes 1376260
  0.6 0.8 copy-start.1
  1.5 14.4 %copy-start.8 = (bf16[8192,16]{0,1:T(8,128)(2,1)S(1)}, bf16[8192,16]{0,1:T(8,128)(2,1)}, u32[]{:S(2)}) copy-start(bf16[8192,16]{0,1:T(8,128)(2,1)} %param.17) | copy-start | bytes 786436
  1.5 14.4 %copy-start.9 = (bf16[8192,16]{0,1:T(8,128)(2,1)S(1)}, bf16[8192,16]{0,1:T(8,128)(2,1)}, u32[]{:S(2)}) copy-start(bf16[8192,16]{0,1:T(8,128)(2,1)} %param.18) | copy-start | bytes 786436
  2.3 29.1 %all-to-all-start = ((bf16[64,2,2048]{2,1,0:T(2,128)(2,1)}), bf16[64,2,2048]{2,1,0:T(2,128)(2,1)S(1)}, u32[]{:S(2)}, u32[]{:S(2)}) async-start(bf16[64,2,2048]{2,1,0:T(2,128)(2,1)} %tokens.1), calls=%async_computation | async-start | bytes 1048576 | tf_op jit(solution)/shard_map/tokens/all_to_all | solution.py:33
  15.9 19.0 %copy-start.5 = (f32[8192]{0:T(1024)S(1)}, f32[8192]{0:T(1024)}, u32[]{:S(2)}) copy-start(f32[8192]{0:T(1024)} %param.20) | copy-start | bytes 98308
  15.9 5.5 %collective-permute-start.4 = (bf16[32,2048]{1,0:T(8,128)(2,1)S(1)}, bf16[32,2048]{1,0:T(8,128)(2,1)S(1)}, u32[]{:S(2)}, u32[]{:S(2)}) collective-permute-start(bf16[32,2048]{1,0:T(8,128)(2,1)S(1)} %bitcast.52), channel_id=1, source_target_pairs={{0,1},{1,0},{2,3},{3,2},{4,5},{5,4},{6,7},{7,6},{8,9},{9,8},{10,11... | collective-permute-start | bytes 393224 | tf_op jit(solution)/shard_map/kv_weights/ppermute | solution.py:45
  17.0 6.1 %collective-permute-start.5 = (bf16[32,2048]{1,0:T(8,128)(2,1)S(1)}, bf16[32,2048]{1,0:T(8,128)(2,1)S(1)}, u32[]{:S(2)}, u32[]{:S(2)}) collective-permute-start(bf16[32,2048]{1,0:T(8,128)(2,1)S(1)} %bitcast.50), channel_id=1, source_target_pairs={{16,0},{32,16},{48,32},{0,48},{17,1},{33,17},{49,33},{1,49},{18,2}... | collective-permute-start | bytes 393224 | tf_op jit(solution)/shard_map/kv_weights/ppermute | solution.py:37
  19.6 7.3 %collective-permute-start.3 = (bf16[32,2048]{1,0:T(8,128)(2,1)S(1)}, bf16[32,2048]{1,0:T(8,128)(2,1)S(1)}, u32[]{:S(2)}, u32[]{:S(2)}) collective-permute-start(bf16[32,2048]{1,0:T(8,128)(2,1)S(1)} %bitcast.49), channel_id=1, source_target_pairs={{48,0},{0,16},{16,32},{32,48},{49,1},{1,17},{17,33},{33,49},{50,2}... | collective-permute-start | bytes 393224 | tf_op jit(solution)/shard_map/kv_weights/ppermute | solution.py:37
  31.6 21.2 %collective-permute-start.1 = (bf16[128,2048]{1,0:T(8,128)(2,1)S(1)}, bf16[128,2048]{1,0:T(8,128)(2,1)S(1)}, u32[]{:S(2)}, u32[]{:S(2)}) collective-permute-start(bf16[128,2048]{1,0:T(8,128)(2,1)S(1)} %reshape.76.mine_ref), channel_id=1, source_target_pairs={{0,1},{1,0},{2,3},{3,2},{4,5},{5,4},{6,7},{7,6},{8,9},{9,8},{10,11... | collective-permute-start | bytes 1572872 | tf_op jit(solution)/shard_map/tokens/ppermute | solution.py:45
  32.4 20.3 %collective-permute-start = (bf16[128,2048]{1,0:T(8,128)(2,1)S(1)}, bf16[128,2048]{1,0:T(8,128)(2,1)S(1)}, u32[]{:S(2)}, u32[]{:S(2)}) collective-permute-start(bf16[128,2048]{1,0:T(8,128)(2,1)S(1)} %reshape.76.mine_ref), channel_id=1, source_target_pairs={{16,0},{32,16},{48,32},{0,48},{17,1},{33,17},{49,33},{1,49},{18,2}... | collective-permute-start | bytes 1572872 | tf_op jit(solution)/shard_map/tokens/ppermute | solution.py:37
  34.9 17.9 %collective-permute-start.2 = (bf16[128,2048]{1,0:T(8,128)(2,1)S(1)}, bf16[128,2048]{1,0:T(8,128)(2,1)S(1)}, u32[]{:S(2)}, u32[]{:S(2)}) collective-permute-start(bf16[128,2048]{1,0:T(8,128)(2,1)S(1)} %reshape.76.mine_ref), channel_id=1, source_target_pairs={{48,0},{0,16},{16,32},{32,48},{49,1},{1,17},{17,33},{33,49},{50,2}... | collective-permute-start | bytes 1572872 | tf_op jit(solution)/shard_map/tokens/ppermute | solution.py:37
  34.9 17.9 %copy-start.2 = (bf16[8192,128]{1,0:T(8,128)(2,1)S(1)}, bf16[8192,128]{1,0:T(8,128)(2,1)}, u32[]{:S(2)}) copy-start(bf16[8192,128]{1,0:T(8,128)(2,1)} %query_weight_ref.1) | copy-start | bytes 6291460
  34.9 17.9 %copy-start.3 = (bf16[128,8192]{1,0:T(8,128)(2,1)S(1)}, bf16[128,8192]{1,0:T(8,128)(2,1)}, u32[]{:S(2)}) copy-start(bf16[128,8192]{1,0:T(8,128)(2,1)} %output_weight_ref.1) | copy-start | bytes 6291460
  34.9 17.9 %copy-start.6 = (s32[1,128]{1,0:T(1,128)S(1)}, s32[1,128]{1,0:T(1,128)}, u32[]{:S(2)}) copy-start(s32[1,128]{1,0:T(1,128)} %seg_ref.1) | copy-start | bytes 1540
  34.9 17.9 %copy-start.7 = (bf16[256,1024]{1,0:T(8,128)(2,1)S(1)}, bf16[256,1024]{1,0:T(8,128)(2,1)}, u32[]{:S(2)}) copy-start(bf16[256,1024]{1,0:T(8,128)(2,1)} %constant.64.clone.pick_ref) | copy-start | bytes 1572868
  54.9 10.6 %collective-permute-start.6 = (bf16[16,128,128]{2,1,0:T(8,128)(2,1)S(1)}, bf16[16,128,128]{2,1,0:T(8,128)(2,1)S(1)}, u32[]{:S(2)}, u32[]{:S(2)}) collective-permute-start(bf16[16,128,128]{2,1,0:T(8,128)(2,1)S(1)} %get-tuple-element.18), channel_id=1, source_target_pairs={{48,0},{0,16},{16,32},{32,48},{49,1},{1,17},{17,33},{33,49},{50,2}... | collective-permute-start | bytes 1572872 | tf_op jit(solution)/shard_map/output/ppermute | solution.py:37
  55.5 10.0 %collective-permute-start.7 = (bf16[16,128,128]{2,1,0:T(8,128)(2,1)S(1)}, bf16[16,128,128]{2,1,0:T(8,128)(2,1)S(1)}, u32[]{:S(2)}, u32[]{:S(2)}) collective-permute-start(bf16[16,128,128]{2,1,0:T(8,128)(2,1)S(1)} %get-tuple-element.19), channel_id=1, source_target_pairs={{0,1},{1,0},{2,3},{3,2},{4,5},{5,4},{6,7},{7,6},{8,9},{9,8},{10,11... | collective-permute-start | bytes 1572872 | tf_op jit(solution)/shard_map/output/ppermute | solution.py:45
  56.1 9.4 %collective-permute-start.8 = (bf16[16,128,128]{2,1,0:T(8,128)(2,1)S(1)}, bf16[16,128,128]{2,1,0:T(8,128)(2,1)S(1)}, u32[]{:S(2)}, u32[]{:S(2)}) collective-permute-start(bf16[16,128,128]{2,1,0:T(8,128)(2,1)S(1)} %get-tuple-element.20), channel_id=1, source_target_pairs={{16,0},{32,16},{48,32},{0,48},{17,1},{33,17},{49,33},{1,49},{18,2}... | collective-permute-start | bytes 1572872 | tf_op jit(solution)/shard_map/output/ppermute | solution.py:37
  65.5 20.5 %copy-start.4 = (bf16[128,3584]{1,0:T(8,128)(2,1)S(1)}, bf16[128,3584]{1,0:T(8,128)(2,1)}, u32[]{:S(2)}) copy-start(bf16[128,3584]{1,0:T(8,128)(2,1)} %projector_ref.1) | copy-start | bytes 2752516
  66.6 19.4 %all-to-all-start.2 = ((bf16[16,128,128]{2,1,0:T(8,128)(2,1)}), bf16[16,128,128]{2,1,0:T(8,128)(2,1)S(1)}, u32[]{:S(2)}, u32[]{:S(2)}) async-start(bf16[16,128,128]{2,1,0:T(8,128)(2,1)} %add_convert_fusion), calls=%async_computation.2 | async-start | bytes 1048576 | tf_op jit(solution)/shard_map/output/all_to_all | solution.py:258
  74.1 15.0 %copy-start.10 = (bf16[2,3584]{1,0:T(2,128)(2,1)S(1)}, bf16[2,3584]{1,0:T(2,128)(2,1)}, u32[]{:S(2)}) copy-start(bf16[2,3584]{1,0:T(2,128)(2,1)} %param.23) | copy-start | bytes 43012
  86.6 5.9 %collective-permute-start.10 = (bf16[32,3712]{1,0:T(8,128)(2,1)S(1)}, bf16[32,3712]{1,0:T(8,128)(2,1)S(1)}, u32[]{:S(2)}, u32[]{:S(2)}) collective-permute-start(bf16[32,3712]{1,0:T(8,128)(2,1)S(1)} %get-tuple-element.23), channel_id=1, source_target_pairs={{0,1},{1,0},{2,3},{3,2},{4,5},{5,4},{6,7},{7,6},{8,9},{9,8},{10,11... | collective-permute-start | bytes 712712 | tf_op jit(solution)/shard_map/target/ppermute | solution.py:45
  86.7 5.8 %collective-permute-start.11 = (bf16[32,3712]{1,0:T(8,128)(2,1)S(1)}, bf16[32,3712]{1,0:T(8,128)(2,1)S(1)}, u32[]{:S(2)}, u32[]{:S(2)}) collective-permute-start(bf16[32,3712]{1,0:T(8,128)(2,1)S(1)} %get-tuple-element.24), channel_id=1, source_target_pairs={{16,0},{32,16},{48,32},{0,48},{17,1},{33,17},{49,33},{1,49},{18,2}... | collective-permute-start | bytes 712712 | tf_op jit(solution)/shard_map/target/ppermute | solution.py:37
  89.1 6.2 %collective-permute-start.9 = (bf16[32,3712]{1,0:T(8,128)(2,1)S(1)}, bf16[32,3712]{1,0:T(8,128)(2,1)S(1)}, u32[]{:S(2)}, u32[]{:S(2)}) collective-permute-start(bf16[32,3712]{1,0:T(8,128)(2,1)S(1)} %get-tuple-element.22), channel_id=1, source_target_pairs={{48,0},{0,16},{16,32},{32,48},{49,1},{1,17},{17,33},{33,49},{50,2}... | collective-permute-start | bytes 712712 | tf_op jit(solution)/shard_map/target/ppermute | solution.py:37
  95.2 6.8 %copy-start.11 = (f32[3584]{0:T(1024)S(1)}, f32[3584]{0:T(1024)}, u32[]{:S(2)}) copy-start(f32[3584]{0:T(1024)} %param.24) | copy-start | bytes 43012
  95.2 6.9 %copy-start.12 = (bf16[3584,64]{0,1:T(8,128)(2,1)S(1)}, bf16[3584,64]{0,1:T(8,128)(2,1)}, u32[]{:S(2)}) copy-start(bf16[3584,64]{0,1:T(8,128)(2,1)} %param.25) | copy-start | bytes 1376260
  96.8 15.3 %all-to-all-start.3 = ((bf16[16,2,3712]{2,1,0:T(2,128)(2,1)}), bf16[16,2,3712]{2,1,0:T(2,128)(2,1)S(1)}, u32[]{:S(2)}, u32[]{:S(2)}) async-start(bf16[16,2,3712]{2,1,0:T(2,128)(2,1)} %reshape.86), calls=%async_computation.3 | async-start | bytes 475136 | tf_op jit(solution)/shard_map/target/all_to_all | solution.py:273
  142.4 4.4 %collective-permute-start.12 = (bf16[128,128]{1,0:T(8,128)(2,1)S(1)}, bf16[128,128]{1,0:T(8,128)(2,1)S(1)}, u32[]{:S(2)}, u32[]{:S(2)}) collective-permute-start(bf16[128,128]{1,0:T(8,128)(2,1)S(1)} %pad_maximum_fusion.2), channel_id=1, source_target_pairs={{4,0},{6,2},{8,4},{10,6},{12,8},{14,10},{0,12},{2,14},{5,1},{7,3},... | collective-permute-start | bytes 98312 | tf_op jit(solution)/shard_map/columns/ppermute | solution.py:41
  143.7 3.1 %collective-permute-start.13 = (bf16[128,128]{1,0:T(8,128)(2,1)S(1)}, bf16[128,128]{1,0:T(8,128)(2,1)S(1)}, u32[]{:S(2)}, u32[]{:S(2)}) collective-permute-start(bf16[128,128]{1,0:T(8,128)(2,1)S(1)} %pad_maximum_fusion.2), channel_id=1, source_target_pairs={{2,0},{4,2},{6,4},{8,6},{10,8},{12,10},{14,12},{0,14},{3,1},{5,3},... | collective-permute-start | bytes 98312 | tf_op jit(solution)/shard_map/columns/ppermute | solution.py:41
  143.7 4.1 %collective-permute-start.14 = (bf16[128,128]{1,0:T(8,128)(2,1)S(1)}, bf16[128,128]{1,0:T(8,128)(2,1)S(1)}, u32[]{:S(2)}, u32[]{:S(2)}) collective-permute-start(bf16[128,128]{1,0:T(8,128)(2,1)S(1)} %pad_maximum_fusion.2), channel_id=1, source_target_pairs={{14,0},{0,2},{2,4},{4,6},{6,8},{8,10},{10,12},{12,14},{15,1},{1,3}... | collective-permute-start | bytes 98312 | tf_op jit(solution)/shard_map/columns/ppermute | solution.py:41
  149.0 21.6 %all-to-all-start.5 = ((bf16[32,128,128]{2,1,0:T(8,128)(2,1)}), bf16[32,128,128]{2,1,0:T(8,128)(2,1)S(1)}, u32[]{:S(2)}, u32[]{:S(2)}) async-start(bf16[32,128,128]{2,1,0:T(8,128)(2,1)} %broadcast_in_dim.8), calls=%async_computation.5 | async-start | bytes 2097152 | tf_op jit(solution)/shard_map/gradients/all_to_all | solution.py:33

commit v2 on v1

--- a/solution.py
+++ b/solution.py
@@ -165,6 +165,17 @@
     return [[c * 8 + quarter + 4 * half for c in range(32) for half in range(2)] for quarter in range(4)]
 
 
+def add_rows(own_ref, one_ref, two_ref, three_ref, out_ref):
+    total = own_ref[...] + one_ref[...].astype(f32) + two_ref[...].astype(f32) + three_ref[...].astype(f32)
+    squares = jnp.sum(total[:, WIDTH:], axis=1, keepdims=True)
+    high = squares.astype(bf16).astype(f32)
+    lane = lax.broadcasted_iota(jnp.int32, (32, 128), 1)
+    tail = jnp.where(lane == 0, high, jnp.where(lane == 1, squares - high, 0.0))
+    total = jnp.concatenate([total[:, :WIDTH], tail], axis=1)
+    for device in range(16):
+        out_ref[device] = total[2 * device : 2 * device + 2].astype(bf16)
+
+
 def spread(tokens_ref, out_ref):
     for colour in range(4):
         block = tokens_ref[:, colour * (D // 4) : (colour + 1) * (D // 4)]
@@ -264,12 +275,14 @@
         total, *sent = vmem_call(
             project, 4, [((32, WIDTH + 128), f32)] + [((32, WIDTH + 128), bf16)] * 3, flops=2**31
         )(where, columns, raw_cols, gain_cols, projector)
-        total = total + from_x(sent[0], 3).astype(f32) + from_yl(sent[1]).astype(f32) + from_x(sent[2], 1).astype(f32)
-        squares = total[:, WIDTH] + total[:, WIDTH + 1]
-        high = squares.astype(bf16)
-        low = (squares - high.astype(f32)).astype(bf16)
-        tail = jnp.pad(jnp.stack([high, low], axis=1), ((0, 0), (0, 126)))
-        rows_out = jnp.concatenate([total[:, :WIDTH].astype(bf16), tail], axis=1).reshape(16, 2, WIDTH + 128)
+        received = from_x(sent[0], 3), from_yl(sent[1]), from_x(sent[2], 1)
+        (rows_out,) = pl.pallas_call(
+            add_rows,
+            out_shape=[jax.ShapeDtypeStruct((16, 2, WIDTH + 128), bf16)],
+            in_specs=[pl.BlockSpec(memory_space=pltpu.VMEM)] * 4,
+            out_specs=[pl.BlockSpec(memory_space=pltpu.VMEM)],
+            compiler_params=pltpu.CompilerParams(vmem_limit_bytes=VMEM_MB * 2**20),
+        )(total, *received)
         rows_in = lax.all_to_all(rows_out, TP, split_axis=0, concat_axis=0, axis_index_groups=same_colour(), tiled=True)
         rows_in = jnp.sum(rows_in.astype(f32), axis=0)
         squares = rows_in[:, WIDTH] + rows_in[:, WIDTH + 1]

time: 173 us -> 172 us (level)
  no operation moved by 1% of the time
where the time goes in v2:
time: 172 us
  waiting for transfers between devices  64.3 us (37%)
  starting transfers between devices  46.6 us (27%)
  blocking collectives  45.9 us (27%)
  local copies, waits for them, and re-layouts  5.16 us (3%)
  Pallas kernels  4.72 us (3%)
  other arithmetic  2.71 us (2%)
    all_to_all x1, blocking collectives, shards(): lax.all_to_all(message, WIDE + ('z',), split_axis=0, concat_axis=0, axis_...  28.4 us
    all_to_all x2, waiting for transfers between devices, exchange(): return lax.all_to_all(blocks, axes, split_axis=0, concat_axis=0, tiled=True)  19.7 us
    all_to_all x2, starting transfers between devices, exchange(): return lax.all_to_all(blocks, axes, split_axis=0, concat_axis=0, tiled=True)  18.9 us
    all_to_all x1, blocking collectives, exchange(): return lax.all_to_all(blocks, axes, split_axis=0, concat_axis=0, tiled=True)  17.5 us
    ppermute x8, waiting for transfers between devices, from_x(): return lax.ppermute(block, 'x', [((i + step) % 4, i) for i in range(4)])  15.4 us
    all_to_all x1, waiting for transfers between devices, shards(): lax.all_to_all(total.astype(bf16), TP, split_axis=0, concat_axis=0, axis_...  11.9 us
    ppermute x8, starting transfers between devices, from_x(): return lax.ppermute(block, 'x', [((i + step) % 4, i) for i in range(4)])  10.3 us
    all_to_all x1, waiting for transfers between devices, shards(): lax.all_to_all(rows_out, TP, split_axis=0, concat_axis=0, axis_index_grou...  9.66 us
  transfers between devices with their start and end apart: 19, of which 12 were waited for; matrix products, arithmetic and copies ran while one was open for 1% of the time, Pallas kernels for 0%

profile of v2, /device:TPU:1, one launch (start us, length us, event | category | flops | bytes accessed | tf_op | source)
XLA Modules:
  0.0 171.8 jit_solution(11789063223634617914)
XLA Ops:
  0.7 0.8 copy-done.1
  1.5 0.8 tokens.1
  2.3 13.5 %all-to-all-start = ((bf16[64,2,2048]{2,1,0:T(2,128)(2,1)}), bf16[64,2,2048]{2,1,0:T(2,128)(2,1)S(1)}, u32[]{:S(2)}, u32[]{:S(2)}) async-start(bf16[64,2,2048]{2,1,0:T(2,128)(2,1)} %tokens.1), calls=%async_computation | async-start | bytes 1048576 | tf_op jit(solution)/shard_map/tokens/all_to_all | solution.py:33
  15.9 1.1 collective-permute-start.4
  17.0 2.6 %collective-permute-start.5 = (bf16[32,2048]{1,0:T(8,128)(2,1)S(1)}, bf16[32,2048]{1,0:T(8,128)(2,1)S(1)}, u32[]{:S(2)}, u32[]{:S(2)}) collective-permute-start(bf16[32,2048]{1,0:T(8,128)(2,1)S(1)} %bitcast.50), channel_id=1, source_target_pairs={{16,0},{32,16},{48,32},{0,48},{17,1},{33,17},{49,33},{1,49},{18,2}... | collective-permute-start | bytes 393224 | tf_op jit(solution)/shard_map/kv_weights/ppermute | solution.py:37
  19.7 1.7 %collective-permute-done.4 = bf16[32,2048]{1,0:T(8,128)(2,1)S(1)} collective-permute-done((bf16[32,2048]{1,0:T(8,128)(2,1)S(1)}, bf16[32,2048]{1,0:T(8,128)(2,1)S(1)}, u32[]{:S(2)}, u32[]{:S(2)}) %collective-permute-start.4) | collective-permute-done | bytes 131104 | tf_op jit(solution)/shard_map/kv_weights/ppermute | solution.py:45
  21.4 1.7 %collective-permute-done.5 = bf16[32,2048]{1,0:T(8,128)(2,1)S(1)} collective-permute-done((bf16[32,2048]{1,0:T(8,128)(2,1)S(1)}, bf16[32,2048]{1,0:T(8,128)(2,1)S(1)}, u32[]{:S(2)}, u32[]{:S(2)}) %collective-permute-start.5) | collective-permute-done | bytes 131104 | tf_op jit(solution)/shard_map/kv_weights/ppermute | solution.py:37
  23.1 3.8 %collective-permute-done.3 = bf16[32,2048]{1,0:T(8,128)(2,1)S(1)} collective-permute-done((bf16[32,2048]{1,0:T(8,128)(2,1)S(1)}, bf16[32,2048]{1,0:T(8,128)(2,1)S(1)}, u32[]{:S(2)}, u32[]{:S(2)}) %collective-permute-start.3) | collective-permute-done | bytes 131104 | tf_op jit(solution)/shard_map/kv_weights/ppermute | solution.py:37
  27.0 0.3 copy.20
  27.3 4.1 %all-to-all-done = bf16[64,2,2048]{2,1,0:T(2,128)(2,1)S(1)} async-done(((bf16[64,2,2048]{2,1,0:T(2,128)(2,1)}), bf16[64,2,2048]{2,1,0:T(2,128)(2,1)S(1)}, u32[]{:S(2)}, u32[]{:S(2)}) %all-to-all-start) | async-done | bytes 524320 | tf_op jit(solution)/shard_map/tokens/all_to_all | solution.py:33
  31.4 0.2 reshape.73.mine_ref
  31.6 0.8 collective-permute-start.1
  32.4 2.4 %collective-permute-start = (bf16[128,2048]{1,0:T(8,128)(2,1)S(1)}, bf16[128,2048]{1,0:T(8,128)(2,1)S(1)}, u32[]{:S(2)}, u32[]{:S(2)}) collective-permute-start(bf16[128,2048]{1,0:T(8,128)(2,1)S(1)} %reshape.73.mine_ref), channel_id=1, source_target_pairs={{16,0},{32,16},{48,32},{0,48},{17,1},{33,17},{49,33},{1,49},{18,2}... | collective-permute-start | bytes 1572872 | tf_op jit(solution)/shard_map/tokens/ppermute | solution.py:37
  34.9 0.3 own_quarter.1
  35.2 17.5 %all_to_all.30 = bf16[64,16,128]{2,1,0:T(8,128)(2,1)S(1)} all-to-all(bf16[64,16,128]{2,1,0:T(8,128)(2,1)S(1)} %own_quarter.1), channel_id=1, replica_groups=mesh['yh'=2,'core'=2,'x'=4,'z'=8,'yl'=2] {'x','z','yl'}, dimensions={0} | all-to-all | bytes 524288 | tf_op jit(solution)/shard_map/own_quarter/all_to_all | solution.py:33
  52.8 2.1 %attention.1 = (f32[16,128,128]{2,1,0:T(8,128)S(1)}, bf16[16,128,128]{2,1,0:T(8,128)(2,1)S(1)}, bf16[16,128,128]{2,1,0:T(8,128)(2,1)S(1)}, bf16[16,128,128]{2,1,0:T(8,128)(2,1)S(1)}) custom-call(s32[1]{0:T(128)} %bitcast.colour_ref, bf16[128,2048]{1,0:T(8,128)(2,1)S(1)} %reshape.73.mine_ref, bf16[128,2048]{1,0:T(8,128)(2,1)S(1)} %collective-permute-done.one_ref, ...), custom_call_target="tpu_custom_call" | custom-call | flops 2147483648 | bytes 4194304 | tf_op jit(solution)/shard_map/attention/attention/pallas_call | solution.py:256
  54.9 0.6 collective-permute-start.6
  55.5 0.6 collective-permute-start.7
  56.1 2.3 %collective-permute-start.8 = (bf16[16,128,128]{2,1,0:T(8,128)(2,1)S(1)}, bf16[16,128,128]{2,1,0:T(8,128)(2,1)S(1)}, u32[]{:S(2)}, u32[]{:S(2)}) collective-permute-start(bf16[16,128,128]{2,1,0:T(8,128)(2,1)S(1)} %get-tuple-element.20), channel_id=1, source_target_pairs={{16,0},{32,16},{48,32},{0,48},{17,1},{33,17},{49,33},{1,49},{18,2}... | collective-permute-start | bytes 1572872 | tf_op jit(solution)/shard_map/output/ppermute | solution.py:37
  58.4 7.1 %collective-permute-done.6 = bf16[16,128,128]{2,1,0:T(8,128)(2,1)S(1)} collective-permute-done((bf16[16,128,128]{2,1,0:T(8,128)(2,1)S(1)}, bf16[16,128,128]{2,1,0:T(8,128)(2,1)S(1)}, u32[]{:S(2)}, u32[]{:S(2)}) %collective-permute-start.6) | collective-permute-done | bytes 524320 | tf_op jit(solution)/shard_map/output/ppermute | solution.py:37
  65.5 1.1 add_convert_fusion
  66.6 6.7 %all-to-all-start.2 = ((bf16[16,128,128]{2,1,0:T(8,128)(2,1)}), bf16[16,128,128]{2,1,0:T(8,128)(2,1)S(1)}, u32[]{:S(2)}, u32[]{:S(2)}) async-start(bf16[16,128,128]{2,1,0:T(8,128)(2,1)} %add_convert_fusion), calls=%async_computation.2 | async-start | bytes 1048576 | tf_op jit(solution)/shard_map/output/all_to_all | solution.py:269
  73.3 0.8 dynamic-slice_bitcast_fusion.gain_ref
  74.1 11.9 %all-to-all-done.2.columns_ref = bf16[16,128,128]{2,1,0:T(8,128)(2,1)S(1)} async-done(((bf16[16,128,128]{2,1,0:T(8,128)(2,1)}), bf16[16,128,128]{2,1,0:T(8,128)(2,1)S(1)}, u32[]{:S(2)}, u32[]{:S(2)}) %all-to-all-start.2) | async-done | bytes 524320 | tf_op jit(solution)/shard_map/output/all_to_all | solution.py:269
  86.0 0.6 project.1
  86.7 2.4 %collective-permute-start.11 = (bf16[32,3712]{1,0:T(8,128)(2,1)S(1)}, bf16[32,3712]{1,0:T(8,128)(2,1)S(1)}, u32[]{:S(2)}, u32[]{:S(2)}) collective-permute-start(bf16[32,3712]{1,0:T(8,128)(2,1)S(1)} %get-tuple-element.24), channel_id=1, source_target_pairs={{16,0},{32,16},{48,32},{0,48},{17,1},{33,17},{49,33},{1,49},{18,2}... | collective-permute-start | bytes 712712 | tf_op jit(solution)/shard_map/target/ppermute | solution.py:37
  89.2 3.3 %collective-permute-done.10.two_ref = bf16[32,3712]{1,0:T(8,128)(2,1)S(1)} collective-permute-done((bf16[32,3712]{1,0:T(8,128)(2,1)S(1)}, bf16[32,3712]{1,0:T(8,128)(2,1)S(1)}, u32[]{:S(2)}, u32[]{:S(2)}) %collective-permute-start.10) | collective-permute-done | bytes 237600 | tf_op jit(solution)/shard_map/target/ppermute | solution.py:45
  92.5 2.7 %collective-permute-done.9.one_ref = bf16[32,3712]{1,0:T(8,128)(2,1)S(1)} collective-permute-done((bf16[32,3712]{1,0:T(8,128)(2,1)S(1)}, bf16[32,3712]{1,0:T(8,128)(2,1)S(1)}, u32[]{:S(2)}, u32[]{:S(2)}) %collective-permute-start.9) | collective-permute-done | bytes 237600 | tf_op jit(solution)/shard_map/target/ppermute | solution.py:37
  95.3 0.9 target.1
  96.1 5.2 %all-to-all-start.3 = ((bf16[16,2,3712]{2,1,0:T(2,128)(2,1)}), bf16[16,2,3712]{2,1,0:T(2,128)(2,1)S(1)}, u32[]{:S(2)}, u32[]{:S(2)}) async-start(bf16[16,2,3712]{2,1,0:T(2,128)(2,1)} %target.1), calls=%async_computation.3 | async-start | bytes 475136 | tf_op jit(solution)/shard_map/target/all_to_all | solution.py:286
  101.5 0.2 convolution_convert_fusion.3
  101.7 9.7 %all-to-all-done.3 = bf16[16,2,3712]{2,1,0:T(2,128)(2,1)S(1)} async-done(((bf16[16,2,3712]{2,1,0:T(2,128)(2,1)}), bf16[16,2,3712]{2,1,0:T(2,128)(2,1)S(1)}, u32[]{:S(2)}, u32[]{:S(2)}) %all-to-all-start.3) | async-done | bytes 237600 | tf_op jit(solution)/shard_map/target/all_to_all | solution.py:286
  111.4 0.2 convert_reduce_fusion
  111.8 0.3 multiply_convert_fusion
  112.1 0.4 convolution_convert_fusion.2
  112.8 28.4 %all_to_all.31 = bf16[64,2,384]{2,1,0:T(2,128)(2,1)S(1)} all-to-all(bf16[64,2,384]{2,1,0:T(2,128)(2,1)S(1)} %bitcast.46), channel_id=1, replica_groups={{0,8,1,9,16,24,17,25,32,40,33,41,48,56,49,57,64,72,65,73,80,88,81,89,96..., dimensions={0} | all-to-all | bytes 196608 | tf_op jit(solution)/shard_map/columns/all_to_all | solution.py:317
  141.3 0.2 convolution_convert_fusion
  141.7 1.3 collective-permute-start.12
  143.0 1.5 collective-permute-start.14
  144.5 1.6 collective-permute-done.12
  146.2 1.0 collective-permute-done.14
  147.2 1.2 broadcast_in_dim.8
  148.4 5.5 %all-to-all-start.5 = ((bf16[32,128,128]{2,1,0:T(8,128)(2,1)}), bf16[32,128,128]{2,1,0:T(8,128)(2,1)S(1)}, u32[]{:S(2)}, u32[]{:S(2)}) async-start(bf16[32,128,128]{2,1,0:T(8,128)(2,1)} %broadcast_in_dim.8), calls=%async_computation.5 | async-start | bytes 2097152 | tf_op jit(solution)/shard_map/gradients/all_to_all | solution.py:33
  153.9 0.5 broadcast_multiply_fusion
  154.4 15.6 %all-to-all-done.5 = bf16[32,128,128]{2,1,0:T(8,128)(2,1)S(1)} async-done(((bf16[32,128,128]{2,1,0:T(8,128)(2,1)}), bf16[32,128,128]{2,1,0:T(8,128)(2,1)S(1)}, u32[]{:S(2)}, u32[]{:S(2)}) %all-to-all-start.5) | async-done | bytes 1048608 | tf_op jit(solution)/shard_map/gradients/all_to_all | solution.py:33
  170.0 0.2 slice_convert_fusion
  170.2 0.2 slice_bitcast_fusion
  170.4 1.4 copy_bitcast_fusion
  (56 shorter events, 1.3 us)
Async XLA Ops:
  0.6 111.2 %copy-start = (bf16[64,3584]{1,0:T(8,128)(2,1)S(1)}, bf16[64,3584]{1,0:T(8,128)(2,1)}, u32[]{:S(2)}) copy-start(bf16[64,3584]{1,0:T(8,128)(2,1)} %param.26) | copy-start | bytes 1376260
  0.6 0.8 copy-start.1
  1.5 14.4 %copy-start.8 = (bf16[8192,16]{0,1:T(8,128)(2,1)S(1)}, bf16[8192,16]{0,1:T(8,128)(2,1)}, u32[]{:S(2)}) copy-start(bf16[8192,16]{0,1:T(8,128)(2,1)} %param.17) | copy-start | bytes 786436
  1.5 14.4 %copy-start.9 = (bf16[8192,16]{0,1:T(8,128)(2,1)S(1)}, bf16[8192,16]{0,1:T(8,128)(2,1)}, u32[]{:S(2)}) copy-start(bf16[8192,16]{0,1:T(8,128)(2,1)} %param.18) | copy-start | bytes 786436
  2.3 29.1 %all-to-all-start = ((bf16[64,2,2048]{2,1,0:T(2,128)(2,1)}), bf16[64,2,2048]{2,1,0:T(2,128)(2,1)S(1)}, u32[]{:S(2)}, u32[]{:S(2)}) async-start(bf16[64,2,2048]{2,1,0:T(2,128)(2,1)} %tokens.1), calls=%async_computation | async-start | bytes 1048576 | tf_op jit(solution)/shard_map/tokens/all_to_all | solution.py:33
  15.9 19.0 %copy-start.5 = (f32[8192]{0:T(1024)S(1)}, f32[8192]{0:T(1024)}, u32[]{:S(2)}) copy-start(f32[8192]{0:T(1024)} %param.20) | copy-start | bytes 98308
  15.9 5.5 %collective-permute-start.4 = (bf16[32,2048]{1,0:T(8,128)(2,1)S(1)}, bf16[32,2048]{1,0:T(8,128)(2,1)S(1)}, u32[]{:S(2)}, u32[]{:S(2)}) collective-permute-start(bf16[32,2048]{1,0:T(8,128)(2,1)S(1)} %bitcast.52), channel_id=1, source_target_pairs={{0,1},{1,0},{2,3},{3,2},{4,5},{5,4},{6,7},{7,6},{8,9},{9,8},{10,11... | collective-permute-start | bytes 393224 | tf_op jit(solution)/shard_map/kv_weights/ppermute | solution.py:45
  17.0 6.1 %collective-permute-start.5 = (bf16[32,2048]{1,0:T(8,128)(2,1)S(1)}, bf16[32,2048]{1,0:T(8,128)(2,1)S(1)}, u32[]{:S(2)}, u32[]{:S(2)}) collective-permute-start(bf16[32,2048]{1,0:T(8,128)(2,1)S(1)} %bitcast.50), channel_id=1, source_target_pairs={{16,0},{32,16},{48,32},{0,48},{17,1},{33,17},{49,33},{1,49},{18,2}... | collective-permute-start | bytes 393224 | tf_op jit(solution)/shard_map/kv_weights/ppermute | solution.py:37
  19.6 7.3 %collective-permute-start.3 = (bf16[32,2048]{1,0:T(8,128)(2,1)S(1)}, bf16[32,2048]{1,0:T(8,128)(2,1)S(1)}, u32[]{:S(2)}, u32[]{:S(2)}) collective-permute-start(bf16[32,2048]{1,0:T(8,128)(2,1)S(1)} %bitcast.49), channel_id=1, source_target_pairs={{48,0},{0,16},{16,32},{32,48},{49,1},{1,17},{17,33},{33,49},{50,2}... | collective-permute-start | bytes 393224 | tf_op jit(solution)/shard_map/kv_weights/ppermute | solution.py:37
  31.6 21.2 %collective-permute-start.1 = (bf16[128,2048]{1,0:T(8,128)(2,1)S(1)}, bf16[128,2048]{1,0:T(8,128)(2,1)S(1)}, u32[]{:S(2)}, u32[]{:S(2)}) collective-permute-start(bf16[128,2048]{1,0:T(8,128)(2,1)S(1)} %reshape.73.mine_ref), channel_id=1, source_target_pairs={{0,1},{1,0},{2,3},{3,2},{4,5},{5,4},{6,7},{7,6},{8,9},{9,8},{10,11... | collective-permute-start | bytes 1572872 | tf_op jit(solution)/shard_map/tokens/ppermute | solution.py:45
  32.4 20.3 %collective-permute-start = (bf16[128,2048]{1,0:T(8,128)(2,1)S(1)}, bf16[128,2048]{1,0:T(8,128)(2,1)S(1)}, u32[]{:S(2)}, u32[]{:S(2)}) collective-permute-start(bf16[128,2048]{1,0:T(8,128)(2,1)S(1)} %reshape.73.mine_ref), channel_id=1, source_target_pairs={{16,0},{32,16},{48,32},{0,48},{17,1},{33,17},{49,33},{1,49},{18,2}... | collective-permute-start | bytes 1572872 | tf_op jit(solution)/shard_map/tokens/ppermute | solution.py:37
  34.9 17.9 %collective-permute-start.2 = (bf16[128,2048]{1,0:T(8,128)(2,1)S(1)}, bf16[128,2048]{1,0:T(8,128)(2,1)S(1)}, u32[]{:S(2)}, u32[]{:S(2)}) collective-permute-start(bf16[128,2048]{1,0:T(8,128)(2,1)S(1)} %reshape.73.mine_ref), channel_id=1, source_target_pairs={{48,0},{0,16},{16,32},{32,48},{49,1},{1,17},{17,33},{33,49},{50,2}... | collective-permute-start | bytes 1572872 | tf_op jit(solution)/shard_map/tokens/ppermute | solution.py:37
  34.9 17.9 %copy-start.2 = (bf16[8192,128]{1,0:T(8,128)(2,1)S(1)}, bf16[8192,128]{1,0:T(8,128)(2,1)}, u32[]{:S(2)}) copy-start(bf16[8192,128]{1,0:T(8,128)(2,1)} %query_weight_ref.1) | copy-start | bytes 6291460
  34.9 17.9 %copy-start.3 = (bf16[128,8192]{1,0:T(8,128)(2,1)S(1)}, bf16[128,8192]{1,0:T(8,128)(2,1)}, u32[]{:S(2)}) copy-start(bf16[128,8192]{1,0:T(8,128)(2,1)} %output_weight_ref.1) | copy-start | bytes 6291460
  34.9 17.9 %copy-start.6 = (s32[1,128]{1,0:T(1,128)S(1)}, s32[1,128]{1,0:T(1,128)}, u32[]{:S(2)}) copy-start(s32[1,128]{1,0:T(1,128)} %seg_ref.1) | copy-start | bytes 1540
  34.9 17.9 %copy-start.7 = (bf16[256,1024]{1,0:T(8,128)(2,1)S(1)}, bf16[256,1024]{1,0:T(8,128)(2,1)}, u32[]{:S(2)}) copy-start(bf16[256,1024]{1,0:T(8,128)(2,1)} %constant.64.clone.pick_ref) | copy-start | bytes 1572868
  54.9 10.6 %collective-permute-start.6 = (bf16[16,128,128]{2,1,0:T(8,128)(2,1)S(1)}, bf16[16,128,128]{2,1,0:T(8,128)(2,1)S(1)}, u32[]{:S(2)}, u32[]{:S(2)}) collective-permute-start(bf16[16,128,128]{2,1,0:T(8,128)(2,1)S(1)} %get-tuple-element.18), channel_id=1, source_target_pairs={{48,0},{0,16},{16,32},{32,48},{49,1},{1,17},{17,33},{33,49},{50,2}... | collective-permute-start | bytes 1572872 | tf_op jit(solution)/shard_map/output/ppermute | solution.py:37
  55.5 10.0 %collective-permute-start.7 = (bf16[16,128,128]{2,1,0:T(8,128)(2,1)S(1)}, bf16[16,128,128]{2,1,0:T(8,128)(2,1)S(1)}, u32[]{:S(2)}, u32[]{:S(2)}) collective-permute-start(bf16[16,128,128]{2,1,0:T(8,128)(2,1)S(1)} %get-tuple-element.19), channel_id=1, source_target_pairs={{0,1},{1,0},{2,3},{3,2},{4,5},{5,4},{6,7},{7,6},{8,9},{9,8},{10,11... | collective-permute-start | bytes 1572872 | tf_op jit(solution)/shard_map/output/ppermute | solution.py:45
  56.1 9.4 %collective-permute-start.8 = (bf16[16,128,128]{2,1,0:T(8,128)(2,1)S(1)}, bf16[16,128,128]{2,1,0:T(8,128)(2,1)S(1)}, u32[]{:S(2)}, u32[]{:S(2)}) collective-permute-start(bf16[16,128,128]{2,1,0:T(8,128)(2,1)S(1)} %get-tuple-element.20), channel_id=1, source_target_pairs={{16,0},{32,16},{48,32},{0,48},{17,1},{33,17},{49,33},{1,49},{18,2}... | collective-permute-start | bytes 1572872 | tf_op jit(solution)/shard_map/output/ppermute | solution.py:37
  65.5 20.5 %copy-start.4 = (bf16[128,3584]{1,0:T(8,128)(2,1)S(1)}, bf16[128,3584]{1,0:T(8,128)(2,1)}, u32[]{:S(2)}) copy-start(bf16[128,3584]{1,0:T(8,128)(2,1)} %projector_ref.1) | copy-start | bytes 2752516
  66.6 19.4 %all-to-all-start.2 = ((bf16[16,128,128]{2,1,0:T(8,128)(2,1)}), bf16[16,128,128]{2,1,0:T(8,128)(2,1)S(1)}, u32[]{:S(2)}, u32[]{:S(2)}) async-start(bf16[16,128,128]{2,1,0:T(8,128)(2,1)} %add_convert_fusion), calls=%async_computation.2 | async-start | bytes 1048576 | tf_op jit(solution)/shard_map/output/all_to_all | solution.py:269
  74.1 15.0 %copy-start.10 = (bf16[2,3584]{1,0:T(2,128)(2,1)S(1)}, bf16[2,3584]{1,0:T(2,128)(2,1)}, u32[]{:S(2)}) copy-start(bf16[2,3584]{1,0:T(2,128)(2,1)} %param.23) | copy-start | bytes 43012
  86.6 14.8 %copy-start.11 = (f32[3584]{0:T(1024)S(1)}, f32[3584]{0:T(1024)}, u32[]{:S(2)}) copy-start(f32[3584]{0:T(1024)} %param.24) | copy-start | bytes 43012
  86.6 14.9 %copy-start.12 = (bf16[3584,64]{0,1:T(8,128)(2,1)S(1)}, bf16[3584,64]{0,1:T(8,128)(2,1)}, u32[]{:S(2)}) copy-start(bf16[3584,64]{0,1:T(8,128)(2,1)} %param.25) | copy-start | bytes 1376260
  86.6 5.9 %collective-permute-start.10 = (bf16[32,3712]{1,0:T(8,128)(2,1)S(1)}, bf16[32,3712]{1,0:T(8,128)(2,1)S(1)}, u32[]{:S(2)}, u32[]{:S(2)}) collective-permute-start(bf16[32,3712]{1,0:T(8,128)(2,1)S(1)} %get-tuple-element.23), channel_id=1, source_target_pairs={{0,1},{1,0},{2,3},{3,2},{4,5},{5,4},{6,7},{7,6},{8,9},{9,8},{10,11... | collective-permute-start | bytes 712712 | tf_op jit(solution)/shard_map/target/ppermute | solution.py:45
  86.7 5.8 %collective-permute-start.11 = (bf16[32,3712]{1,0:T(8,128)(2,1)S(1)}, bf16[32,3712]{1,0:T(8,128)(2,1)S(1)}, u32[]{:S(2)}, u32[]{:S(2)}) collective-permute-start(bf16[32,3712]{1,0:T(8,128)(2,1)S(1)} %get-tuple-element.24), channel_id=1, source_target_pairs={{16,0},{32,16},{48,32},{0,48},{17,1},{33,17},{49,33},{1,49},{18,2}... | collective-permute-start | bytes 712712 | tf_op jit(solution)/shard_map/target/ppermute | solution.py:37
  89.1 6.2 %collective-permute-start.9 = (bf16[32,3712]{1,0:T(8,128)(2,1)S(1)}, bf16[32,3712]{1,0:T(8,128)(2,1)S(1)}, u32[]{:S(2)}, u32[]{:S(2)}) collective-permute-start(bf16[32,3712]{1,0:T(8,128)(2,1)S(1)} %get-tuple-element.22), channel_id=1, source_target_pairs={{48,0},{0,16},{16,32},{32,48},{49,1},{1,17},{17,33},{33,49},{50,2}... | collective-permute-start | bytes 712712 | tf_op jit(solution)/shard_map/target/ppermute | solution.py:37
  96.1 15.3 %all-to-all-start.3 = ((bf16[16,2,3712]{2,1,0:T(2,128)(2,1)}), bf16[16,2,3712]{2,1,0:T(2,128)(2,1)S(1)}, u32[]{:S(2)}, u32[]{:S(2)}) async-start(bf16[16,2,3712]{2,1,0:T(2,128)(2,1)} %target.1), calls=%async_computation.3 | async-start | bytes 475136 | tf_op jit(solution)/shard_map/target/all_to_all | solution.py:286
  141.7 4.4 %collective-permute-start.12 = (bf16[128,128]{1,0:T(8,128)(2,1)S(1)}, bf16[128,128]{1,0:T(8,128)(2,1)S(1)}, u32[]{:S(2)}, u32[]{:S(2)}) collective-permute-start(bf16[128,128]{1,0:T(8,128)(2,1)S(1)} %pad_maximum_fusion.2), channel_id=1, source_target_pairs={{4,0},{6,2},{8,4},{10,6},{12,8},{14,10},{0,12},{2,14},{5,1},{7,3},... | collective-permute-start | bytes 98312 | tf_op jit(solution)/shard_map/columns/ppermute | solution.py:41
  143.0 3.1 %collective-permute-start.13 = (bf16[128,128]{1,0:T(8,128)(2,1)S(1)}, bf16[128,128]{1,0:T(8,128)(2,1)S(1)}, u32[]{:S(2)}, u32[]{:S(2)}) collective-permute-start(bf16[128,128]{1,0:T(8,128)(2,1)S(1)} %pad_maximum_fusion.2), channel_id=1, source_target_pairs={{2,0},{4,2},{6,4},{8,6},{10,8},{12,10},{14,12},{0,14},{3,1},{5,3},... | collective-permute-start | bytes 98312 | tf_op jit(solution)/shard_map/columns/ppermute | solution.py:41
  143.0 4.1 %collective-permute-start.14 = (bf16[128,128]{1,0:T(8,128)(2,1)S(1)}, bf16[128,128]{1,0:T(8,128)(2,1)S(1)}, u32[]{:S(2)}, u32[]{:S(2)}) collective-permute-start(bf16[128,128]{1,0:T(8,128)(2,1)S(1)} %pad_maximum_fusion.2), channel_id=1, source_target_pairs={{14,0},{0,2},{2,4},{4,6},{6,8},{8,10},{10,12},{12,14},{15,1},{1,3}... | collective-permute-start | bytes 98312 | tf_op jit(solution)/shard_map/columns/ppermute | solution.py:41
  148.4 21.6 %all-to-all-start.5 = ((bf16[32,128,128]{2,1,0:T(8,128)(2,1)}), bf16[32,128,128]{2,1,0:T(8,128)(2,1)S(1)}, u32[]{:S(2)}, u32[]{:S(2)}) async-start(bf16[32,128,128]{2,1,0:T(8,128)(2,1)} %broadcast_in_dim.8), calls=%async_computation.5 | async-start | bytes 2097152 | tf_op jit(solution)/shard_map/gradients/all_to_all | solution.py:33

commit v3 on v2

--- a/solution.py
+++ b/solution.py
@@ -119,7 +119,7 @@
             at = pl.multiple_of(start_of(step) + z * 256, 256)
             product = jnp.dot(context, output_weight_ref[:, pl.ds(at, 256)], preferred_element_type=f32)
             for yl in range(2):
-                ref = refs[(step + 2 * yl) % 4]
+                ref = refs[(step + 2 * yl + z) % 4]
                 ref[yl * 8 + z] = product[:, yl * 128 : yl * 128 + 128].astype(ref.dtype)
 
 
@@ -138,8 +138,9 @@
     features = (resid * gain_ref[...]).astype(bf16)
     row = lax.broadcasted_iota(jnp.int32, (128, 128), 0)
     yl = (row >> 4) & 1
-    x = (colour_ref[0] + (row >> 5) + 2 * yl) & 3
-    token = 32 * x + 4 * ((row >> 1) & 7) + 2 * yl + (row & 1)
+    z = (row >> 1) & 7
+    x = (colour_ref[0] + (row >> 5) + 2 * yl + 8 - z) & 3
+    token = 32 * x + 4 * z + 2 * yl + (row & 1)
     order = jnp.where(lane == token, 1.0, 0.0).astype(bf16)
     features = jnp.dot(order, features, preferred_element_type=f32).astype(bf16)
     tail = jnp.dot(order, tail, preferred_element_type=f32)
@@ -156,9 +157,7 @@
     def index(x, z, yl):
         return x * 16 + z * 2 + yl
 
-    return [
-        [index(c, z, 0) for z in range(8)] + [index((c + 2) % 4, z, 1) for z in range(8)] for c in range(4)
-    ]
+    return [[index((c + 2 * yl - z) % 4, z, yl) for yl in range(2) for z in range(8)] for c in range(4)]
 
 
 def same_quarter():
@@ -181,7 +180,7 @@
         block = tokens_ref[:, colour * (D // 4) : (colour + 1) * (D // 4)]
         for z in range(8):
             for yl in range(2):
-                out_ref[(colour + 2 * yl) % 4 * 16 + z * 2 + yl] = block
+                out_ref[(colour + 2 * yl - z) % 4 * 16 + z * 2 + yl] = block
 
 
 def vmem_call(kernel, ins, outs, flops):
@@ -213,7 +212,7 @@
     adapter_up_map,
 ):
     tp_index = lax.axis_index(TP)
-    colour = lax.rem(lax.axis_index("x") + 2 * lax.axis_index("yl"), 4)
+    colour = lax.rem(lax.axis_index("x") + 2 * lax.axis_index("yl") + lax.axis_index("z"), 4)
 
     with jax.named_scope("tokens"):
         (by_colour,) = pl.pallas_call(
@@ -229,11 +228,8 @@
         mine = exchange(by_colour, TP).reshape(128, D // 4)
         parts = [mine, from_x(mine, 1), from_yl(mine), from_x(mine, 3)]
         at = lax.rem(tp_index, 16) * HD
-        raw_cols = jnp.where(
-            lax.axis_index("yl") == 0,
-            lax.dynamic_slice_in_dim(parts[0], at, HD, 1),
-            lax.dynamic_slice_in_dim(parts[2], at, HD, 1),
-        )
+        step = lax.rem(lax.axis_index("x") + 4 - colour, 4)
+        raw_cols = lax.select_n(step, *[lax.dynamic_slice_in_dim(part, at, HD, 1) for part in parts])
 
     with jax.named_scope("kv_weights"):
         columns = jnp.stack([key_columns.T, value_columns.T]).reshape(2, 2, KV, D)

time: 172 us -> 172 us (level)
  waiting for transfers between devices: 64.3 us -> 60 us
  starting transfers between devices: 46.6 us -> 50.1 us
    ppermute x4, waiting for transfers between devices: 5.02 us -> 0.01 us  [from_yl(): return lax.ppermute(block, 'yl', [(0, 1), (1, 0)])]
    all_to_all x2, waiting for transfers between devices: 19.7 us -> 22.9 us  [exchange(): return lax.all_to_all(blocks, axes, split_axis=0, concat_axis=0, tiled=True)]
    all_to_all x1, starting transfers between devices: 5.25 us -> 6.98 us  [shards(): lax.all_to_all(rows_out, TP, split_axis=0, concat_axis=0, axis_index_grou...]
  transfers between devices with their start and end apart: 19 -> 19, of which waited for: 12 -> 11; matrix products, arithmetic and copies ran while one was open for 1% -> 1% of each run, Pallas kernels for 0% -> 0%
where the time goes in v3:
time: 172 us; the launch traced here: 171 us
  waiting for transfers between devices  60 us (35%)
  starting transfers between devices  50.1 us (29%)
  blocking collectives  44.9 us (26%)
  local copies, waits for them, and re-layouts  6.33 us (4%)
  Pallas kernels  4.68 us (3%)
  other arithmetic  2.75 us (2%)
    all_to_all x1, blocking collectives, shards(): lax.all_to_all(message, WIDE + ('z',), split_axis=0, concat_axis=0, axis_...  27.9 us
    all_to_all x2, waiting for transfers between devices, exchange(): return lax.all_to_all(blocks, axes, split_axis=0, concat_axis=0, tiled=True)  22.9 us
    all_to_all x2, starting transfers between devices, exchange(): return lax.all_to_all(blocks, axes, split_axis=0, concat_axis=0, tiled=True)  19 us
    all_to_all x1, blocking collectives, exchange(): return lax.all_to_all(blocks, axes, split_axis=0, concat_axis=0, tiled=True)  17 us
    ppermute x8, waiting for transfers between devices, from_x(): return lax.ppermute(block, 'x', [((i + step) % 4, i) for i in range(4)])  14.2 us
    ppermute x8, starting transfers between devices, from_x(): return lax.ppermute(block, 'x', [((i + step) % 4, i) for i in range(4)])  10.7 us
    all_to_all x1, waiting for transfers between devices, shards(): lax.all_to_all(total.astype(bf16), TP, split_axis=0, concat_axis=0, axis_...  10.6 us
    all_to_all x1, waiting for transfers between devices, shards(): lax.all_to_all(rows_out, TP, split_axis=0, concat_axis=0, axis_index_grou...  9.57 us
  transfers between devices with their start and end apart: 19, of which 11 were waited for; matrix products, arithmetic and copies ran while one was open for 1% of the time, Pallas kernels for 0%

profile of v3, /device:TPU:1, one launch (start us, length us, event | category | flops | bytes accessed | tf_op | source)
XLA Modules:
  0.0 171.1 jit_solution(978607730180724452)
XLA Ops:
  0.7 0.8 copy-done.1
  1.5 0.8 tokens.1
  2.3 13.5 %all-to-all-start = ((bf16[64,2,2048]{2,1,0:T(2,128)(2,1)}), bf16[64,2,2048]{2,1,0:T(2,128)(2,1)S(1)}, u32[]{:S(2)}, u32[]{:S(2)}) async-start(bf16[64,2,2048]{2,1,0:T(2,128)(2,1)} %tokens.1), calls=%async_computation | async-start | bytes 1048576 | tf_op jit(solution)/shard_map/tokens/all_to_all | solution.py:33
  15.9 1.1 collective-permute-start.3
  17.0 1.2 collective-permute-start.4
  18.2 1.5 collective-permute-start.5
  19.7 2.3 %collective-permute-done.3 = bf16[32,2048]{1,0:T(8,128)(2,1)S(1)} collective-permute-done((bf16[32,2048]{1,0:T(8,128)(2,1)S(1)}, bf16[32,2048]{1,0:T(8,128)(2,1)S(1)}, u32[]{:S(2)}, u32[]{:S(2)}) %collective-permute-start.3) | collective-permute-done | bytes 131104 | tf_op jit(solution)/shard_map/kv_weights/ppermute | solution.py:37
  22.0 1.7 collective-permute-done.5
  23.7 0.3 copy.20
  24.0 7.3 %all-to-all-done = bf16[64,2,2048]{2,1,0:T(2,128)(2,1)S(1)} async-done(((bf16[64,2,2048]{2,1,0:T(2,128)(2,1)}), bf16[64,2,2048]{2,1,0:T(2,128)(2,1)S(1)}, u32[]{:S(2)}, u32[]{:S(2)}) %all-to-all-start) | async-done | bytes 524320 | tf_op jit(solution)/shard_map/tokens/all_to_all | solution.py:33
  31.6 0.8 collective-permute-start.2
  32.3 1.0 collective-permute-start.1
  33.3 1.8 %collective-permute-start = (bf16[128,2048]{1,0:T(8,128)(2,1)S(1)}, bf16[128,2048]{1,0:T(8,128)(2,1)S(1)}, u32[]{:S(2)}, u32[]{:S(2)}) collective-permute-start(bf16[128,2048]{1,0:T(8,128)(2,1)S(1)} %reshape.73.mine_ref), channel_id=1, source_target_pairs={{16,0},{32,16},{48,32},{0,48},{17,1},{33,17},{49,33},{1,49},{18,2}... | collective-permute-start | bytes 1572872 | tf_op jit(solution)/shard_map/tokens/ppermute | solution.py:37
  35.1 0.3 own_quarter.1
  35.4 17.0 %all_to_all.30 = bf16[64,16,128]{2,1,0:T(8,128)(2,1)S(1)} all-to-all(bf16[64,16,128]{2,1,0:T(8,128)(2,1)S(1)} %own_quarter.1), channel_id=1, replica_groups=mesh['yh'=2,'core'=2,'x'=4,'z'=8,'yl'=2] {'x','z','yl'}, dimensions={0} | all-to-all | bytes 524288 | tf_op jit(solution)/shard_map/own_quarter/all_to_all | solution.py:33
  52.5 2.1 %attention.1 = (f32[16,128,128]{2,1,0:T(8,128)S(1)}, bf16[16,128,128]{2,1,0:T(8,128)(2,1)S(1)}, bf16[16,128,128]{2,1,0:T(8,128)(2,1)S(1)}, bf16[16,128,128]{2,1,0:T(8,128)(2,1)S(1)}) custom-call(s32[1]{0:T(128)} %bitcast.colour_ref, bf16[128,2048]{1,0:T(8,128)(2,1)S(1)} %reshape.73.mine_ref, bf16[128,2048]{1,0:T(8,128)(2,1)S(1)} %collective-permute-done.one_ref, ...), custom_call_target="tpu_custom_call" | custom-call | flops 2147483648 | bytes 4194304 | tf_op jit(solution)/shard_map/attention/attention/pallas_call | solution.py:252
  54.6 0.5 collective-permute-start.6
  55.1 0.7 collective-permute-start.7
  55.8 2.2 %collective-permute-start.8 = (bf16[16,128,128]{2,1,0:T(8,128)(2,1)S(1)}, bf16[16,128,128]{2,1,0:T(8,128)(2,1)S(1)}, u32[]{:S(2)}, u32[]{:S(2)}) collective-permute-start(bf16[16,128,128]{2,1,0:T(8,128)(2,1)S(1)} %get-tuple-element.20), channel_id=1, source_target_pairs={{16,0},{32,16},{48,32},{0,48},{17,1},{33,17},{49,33},{1,49},{18,2}... | collective-permute-start | bytes 1572872 | tf_op jit(solution)/shard_map/output/ppermute | solution.py:37
  58.0 7.2 %collective-permute-done.6 = bf16[16,128,128]{2,1,0:T(8,128)(2,1)S(1)} collective-permute-done((bf16[16,128,128]{2,1,0:T(8,128)(2,1)S(1)}, bf16[16,128,128]{2,1,0:T(8,128)(2,1)S(1)}, u32[]{:S(2)}, u32[]{:S(2)}) %collective-permute-start.6) | collective-permute-done | bytes 524320 | tf_op jit(solution)/shard_map/output/ppermute | solution.py:37
  65.2 1.1 add_convert_fusion
  66.4 7.3 %all-to-all-start.2 = ((bf16[16,128,128]{2,1,0:T(8,128)(2,1)}), bf16[16,128,128]{2,1,0:T(8,128)(2,1)S(1)}, u32[]{:S(2)}, u32[]{:S(2)}) async-start(bf16[16,128,128]{2,1,0:T(8,128)(2,1)} %add_convert_fusion), calls=%async_computation.2 | async-start | bytes 1048576 | tf_op jit(solution)/shard_map/output/all_to_all | solution.py:265
  73.7 0.8 dynamic-slice_bitcast_fusion.gain_ref
  74.5 10.6 %all-to-all-done.2.columns_ref = bf16[16,128,128]{2,1,0:T(8,128)(2,1)S(1)} async-done(((bf16[16,128,128]{2,1,0:T(8,128)(2,1)}), bf16[16,128,128]{2,1,0:T(8,128)(2,1)S(1)}, u32[]{:S(2)}, u32[]{:S(2)}) %all-to-all-start.2) | async-done | bytes 524320 | tf_op jit(solution)/shard_map/output/all_to_all | solution.py:265
  85.1 1.2 copy-done.4
  86.3 0.6 project.1
  86.9 0.5 collective-permute-start.9
  87.3 0.5 collective-permute-start.10
  87.9 2.4 %collective-permute-start.11 = (bf16[32,3712]{1,0:T(8,128)(2,1)S(1)}, bf16[32,3712]{1,0:T(8,128)(2,1)S(1)}, u32[]{:S(2)}, u32[]{:S(2)}) collective-permute-start(bf16[32,3712]{1,0:T(8,128)(2,1)S(1)} %get-tuple-element.24), channel_id=1, source_target_pairs={{16,0},{32,16},{48,32},{0,48},{17,1},{33,17},{49,33},{1,49},{18,2}... | collective-permute-start | bytes 712712 | tf_op jit(solution)/shard_map/target/ppermute | solution.py:37
  90.4 3.1 %collective-permute-done.9.one_ref = bf16[32,3712]{1,0:T(8,128)(2,1)S(1)} collective-permute-done((bf16[32,3712]{1,0:T(8,128)(2,1)S(1)}, bf16[32,3712]{1,0:T(8,128)(2,1)S(1)}, u32[]{:S(2)}, u32[]{:S(2)}) %collective-permute-start.9) | collective-permute-done | bytes 237600 | tf_op jit(solution)/shard_map/target/ppermute | solution.py:37
  93.5 0.9 target.1
  94.4 7.0 %all-to-all-start.3 = ((bf16[16,2,3712]{2,1,0:T(2,128)(2,1)}), bf16[16,2,3712]{2,1,0:T(2,128)(2,1)S(1)}, u32[]{:S(2)}, u32[]{:S(2)}) async-start(bf16[16,2,3712]{2,1,0:T(2,128)(2,1)} %target.1), calls=%async_computation.3 | async-start | bytes 475136 | tf_op jit(solution)/shard_map/target/all_to_all | solution.py:282
  101.5 0.2 convolution_convert_fusion.3
  101.7 9.6 %all-to-all-done.3 = bf16[16,2,3712]{2,1,0:T(2,128)(2,1)S(1)} async-done(((bf16[16,2,3712]{2,1,0:T(2,128)(2,1)}), bf16[16,2,3712]{2,1,0:T(2,128)(2,1)S(1)}, u32[]{:S(2)}, u32[]{:S(2)}) %all-to-all-start.3) | async-done | bytes 237600 | tf_op jit(solution)/shard_map/target/all_to_all | solution.py:282
  111.7 0.3 multiply_convert_fusion
  111.9 0.5 convolution_convert_fusion.2
  112.7 27.9 %all_to_all.31 = bf16[64,2,384]{2,1,0:T(2,128)(2,1)S(1)} all-to-all(bf16[64,2,384]{2,1,0:T(2,128)(2,1)S(1)} %bitcast.46), channel_id=1, replica_groups={{0,8,1,9,16,24,17,25,32,40,33,41,48,56,49,57,64,72,65,73,80,88,81,89,96..., dimensions={0} | all-to-all | bytes 196608 | tf_op jit(solution)/shard_map/columns/all_to_all | solution.py:313
  140.8 0.2 convolution_convert_fusion
  141.0 1.1 collective-permute-start.13
  142.4 1.4 collective-permute-start.14
  143.9 2.0 %collective-permute-done.12 = bf16[128,128]{1,0:T(8,128)(2,1)S(1)} collective-permute-done((bf16[128,128]{1,0:T(8,128)(2,1)S(1)}, bf16[128,128]{1,0:T(8,128)(2,1)S(1)}, u32[]{:S(2)}, u32[]{:S(2)}) %collective-permute-start.12) | collective-permute-done | bytes 32800 | tf_op jit(solution)/shard_map/columns/ppermute | solution.py:41
  145.8 0.5 collective-permute-done.14
  146.4 1.2 broadcast_in_dim.8
  147.6 5.5 %all-to-all-start.5 = ((bf16[32,128,128]{2,1,0:T(8,128)(2,1)}), bf16[32,128,128]{2,1,0:T(8,128)(2,1)S(1)}, u32[]{:S(2)}, u32[]{:S(2)}) async-start(bf16[32,128,128]{2,1,0:T(8,128)(2,1)} %broadcast_in_dim.8), calls=%async_computation.5 | async-start | bytes 2097152 | tf_op jit(solution)/shard_map/gradients/all_to_all | solution.py:33
  153.1 0.5 broadcast_multiply_fusion
  153.7 15.6 %all-to-all-done.5 = bf16[32,128,128]{2,1,0:T(8,128)(2,1)S(1)} async-done(((bf16[32,128,128]{2,1,0:T(8,128)(2,1)}), bf16[32,128,128]{2,1,0:T(8,128)(2,1)S(1)}, u32[]{:S(2)}, u32[]{:S(2)}) %all-to-all-start.5) | async-done | bytes 1048608 | tf_op jit(solution)/shard_map/gradients/all_to_all | solution.py:33
  169.4 0.2 slice_bitcast_fusion
  169.7 1.4 copy_bitcast_fusion
  (56 shorter events, 2.1 us)
Async XLA Ops:
  0.6 111.0 %copy-start = (bf16[64,3584]{1,0:T(8,128)(2,1)S(1)}, bf16[64,3584]{1,0:T(8,128)(2,1)}, u32[]{:S(2)}) copy-start(bf16[64,3584]{1,0:T(8,128)(2,1)} %param.26) | copy-start | bytes 1376260
  0.6 0.8 copy-start.1
  1.5 14.4 %copy-start.8 = (bf16[8192,16]{0,1:T(8,128)(2,1)S(1)}, bf16[8192,16]{0,1:T(8,128)(2,1)}, u32[]{:S(2)}) copy-start(bf16[8192,16]{0,1:T(8,128)(2,1)} %param.17) | copy-start | bytes 786436
  1.5 14.4 %copy-start.9 = (bf16[8192,16]{0,1:T(8,128)(2,1)S(1)}, bf16[8192,16]{0,1:T(8,128)(2,1)}, u32[]{:S(2)}) copy-start(bf16[8192,16]{0,1:T(8,128)(2,1)} %param.18) | copy-start | bytes 786436
  2.3 29.1 %all-to-all-start = ((bf16[64,2,2048]{2,1,0:T(2,128)(2,1)}), bf16[64,2,2048]{2,1,0:T(2,128)(2,1)S(1)}, u32[]{:S(2)}, u32[]{:S(2)}) async-start(bf16[64,2,2048]{2,1,0:T(2,128)(2,1)} %tokens.1), calls=%async_computation | async-start | bytes 1048576 | tf_op jit(solution)/shard_map/tokens/all_to_all | solution.py:33
  15.9 19.2 %copy-start.5 = (f32[8192]{0:T(1024)S(1)}, f32[8192]{0:T(1024)}, u32[]{:S(2)}) copy-start(f32[8192]{0:T(1024)} %param.20) | copy-start | bytes 98308
  15.9 6.1 %collective-permute-start.3 = (bf16[32,2048]{1,0:T(8,128)(2,1)S(1)}, bf16[32,2048]{1,0:T(8,128)(2,1)S(1)}, u32[]{:S(2)}, u32[]{:S(2)}) collective-permute-start(bf16[32,2048]{1,0:T(8,128)(2,1)S(1)} %bitcast.52), channel_id=1, source_target_pairs={{48,0},{0,16},{16,32},{32,48},{49,1},{1,17},{17,33},{33,49},{50,2}... | collective-permute-start | bytes 393224 | tf_op jit(solution)/shard_map/kv_weights/ppermute | solution.py:37
  17.0 5.0 %collective-permute-start.4 = (bf16[32,2048]{1,0:T(8,128)(2,1)S(1)}, bf16[32,2048]{1,0:T(8,128)(2,1)S(1)}, u32[]{:S(2)}, u32[]{:S(2)}) collective-permute-start(bf16[32,2048]{1,0:T(8,128)(2,1)S(1)} %bitcast.50), channel_id=1, source_target_pairs={{0,1},{1,0},{2,3},{3,2},{4,5},{5,4},{6,7},{7,6},{8,9},{9,8},{10,11... | collective-permute-start | bytes 393224 | tf_op jit(solution)/shard_map/kv_weights/ppermute | solution.py:45
  18.2 5.5 %collective-permute-start.5 = (bf16[32,2048]{1,0:T(8,128)(2,1)S(1)}, bf16[32,2048]{1,0:T(8,128)(2,1)S(1)}, u32[]{:S(2)}, u32[]{:S(2)}) collective-permute-start(bf16[32,2048]{1,0:T(8,128)(2,1)S(1)} %bitcast.49), channel_id=1, source_target_pairs={{16,0},{32,16},{48,32},{0,48},{17,1},{33,17},{49,33},{1,49},{18,2}... | collective-permute-start | bytes 393224 | tf_op jit(solution)/shard_map/kv_weights/ppermute | solution.py:37
  31.6 20.9 %collective-permute-start.2 = (bf16[128,2048]{1,0:T(8,128)(2,1)S(1)}, bf16[128,2048]{1,0:T(8,128)(2,1)S(1)}, u32[]{:S(2)}, u32[]{:S(2)}) collective-permute-start(bf16[128,2048]{1,0:T(8,128)(2,1)S(1)} %reshape.73.mine_ref), channel_id=1, source_target_pairs={{48,0},{0,16},{16,32},{32,48},{49,1},{1,17},{17,33},{33,49},{50,2}... | collective-permute-start | bytes 1572872 | tf_op jit(solution)/shard_map/tokens/ppermute | solution.py:37
  32.3 20.1 %collective-permute-start.1 = (bf16[128,2048]{1,0:T(8,128)(2,1)S(1)}, bf16[128,2048]{1,0:T(8,128)(2,1)S(1)}, u32[]{:S(2)}, u32[]{:S(2)}) collective-permute-start(bf16[128,2048]{1,0:T(8,128)(2,1)S(1)} %reshape.73.mine_ref), channel_id=1, source_target_pairs={{0,1},{1,0},{2,3},{3,2},{4,5},{5,4},{6,7},{7,6},{8,9},{9,8},{10,11... | collective-permute-start | bytes 1572872 | tf_op jit(solution)/shard_map/tokens/ppermute | solution.py:45
  33.3 19.1 %collective-permute-start = (bf16[128,2048]{1,0:T(8,128)(2,1)S(1)}, bf16[128,2048]{1,0:T(8,128)(2,1)S(1)}, u32[]{:S(2)}, u32[]{:S(2)}) collective-permute-start(bf16[128,2048]{1,0:T(8,128)(2,1)S(1)} %reshape.73.mine_ref), channel_id=1, source_target_pairs={{16,0},{32,16},{48,32},{0,48},{17,1},{33,17},{49,33},{1,49},{18,2}... | collective-permute-start | bytes 1572872 | tf_op jit(solution)/shard_map/tokens/ppermute | solution.py:37
  35.1 17.3 %copy-start.2 = (bf16[8192,128]{1,0:T(8,128)(2,1)S(1)}, bf16[8192,128]{1,0:T(8,128)(2,1)}, u32[]{:S(2)}) copy-start(bf16[8192,128]{1,0:T(8,128)(2,1)} %query_weight_ref.1) | copy-start | bytes 6291460
  35.1 17.4 %copy-start.3 = (bf16[128,8192]{1,0:T(8,128)(2,1)S(1)}, bf16[128,8192]{1,0:T(8,128)(2,1)}, u32[]{:S(2)}) copy-start(bf16[128,8192]{1,0:T(8,128)(2,1)} %output_weight_ref.1) | copy-start | bytes 6291460
  35.1 17.4 %copy-start.6 = (s32[1,128]{1,0:T(1,128)S(1)}, s32[1,128]{1,0:T(1,128)}, u32[]{:S(2)}) copy-start(s32[1,128]{1,0:T(1,128)} %seg_ref.1) | copy-start | bytes 1540
  35.1 17.4 %copy-start.7 = (bf16[256,1024]{1,0:T(8,128)(2,1)S(1)}, bf16[256,1024]{1,0:T(8,128)(2,1)}, u32[]{:S(2)}) copy-start(bf16[256,1024]{1,0:T(8,128)(2,1)} %constant.67.clone.pick_ref) | copy-start | bytes 1572868
  54.6 10.7 %collective-permute-start.6 = (bf16[16,128,128]{2,1,0:T(8,128)(2,1)S(1)}, bf16[16,128,128]{2,1,0:T(8,128)(2,1)S(1)}, u32[]{:S(2)}, u32[]{:S(2)}) collective-permute-start(bf16[16,128,128]{2,1,0:T(8,128)(2,1)S(1)} %get-tuple-element.18), channel_id=1, source_target_pairs={{48,0},{0,16},{16,32},{32,48},{49,1},{1,17},{17,33},{33,49},{50,2}... | collective-permute-start | bytes 1572872 | tf_op jit(solution)/shard_map/output/ppermute | solution.py:37
  55.1 10.2 %collective-permute-start.7 = (bf16[16,128,128]{2,1,0:T(8,128)(2,1)S(1)}, bf16[16,128,128]{2,1,0:T(8,128)(2,1)S(1)}, u32[]{:S(2)}, u32[]{:S(2)}) collective-permute-start(bf16[16,128,128]{2,1,0:T(8,128)(2,1)S(1)} %get-tuple-element.19), channel_id=1, source_target_pairs={{0,1},{1,0},{2,3},{3,2},{4,5},{5,4},{6,7},{7,6},{8,9},{9,8},{10,11... | collective-permute-start | bytes 1572872 | tf_op jit(solution)/shard_map/output/ppermute | solution.py:45
  55.8 9.5 %collective-permute-start.8 = (bf16[16,128,128]{2,1,0:T(8,128)(2,1)S(1)}, bf16[16,128,128]{2,1,0:T(8,128)(2,1)S(1)}, u32[]{:S(2)}, u32[]{:S(2)}) collective-permute-start(bf16[16,128,128]{2,1,0:T(8,128)(2,1)S(1)} %get-tuple-element.20), channel_id=1, source_target_pairs={{16,0},{32,16},{48,32},{0,48},{17,1},{33,17},{49,33},{1,49},{18,2}... | collective-permute-start | bytes 1572872 | tf_op jit(solution)/shard_map/output/ppermute | solution.py:37
  66.4 18.7 %all-to-all-start.2 = ((bf16[16,128,128]{2,1,0:T(8,128)(2,1)}), bf16[16,128,128]{2,1,0:T(8,128)(2,1)S(1)}, u32[]{:S(2)}, u32[]{:S(2)}) async-start(bf16[16,128,128]{2,1,0:T(8,128)(2,1)} %add_convert_fusion), calls=%async_computation.2 | async-start | bytes 1048576 | tf_op jit(solution)/shard_map/output/all_to_all | solution.py:265
  85.1 1.2 copy-start.4
  86.3 4.0 %copy-start.10 = (bf16[2,3584]{1,0:T(2,128)(2,1)S(1)}, bf16[2,3584]{1,0:T(2,128)(2,1)}, u32[]{:S(2)}) copy-start(bf16[2,3584]{1,0:T(2,128)(2,1)} %param.23) | copy-start | bytes 43012
  86.8 14.5 %copy-start.11 = (f32[3584]{0:T(1024)S(1)}, f32[3584]{0:T(1024)}, u32[]{:S(2)}) copy-start(f32[3584]{0:T(1024)} %param.24) | copy-start | bytes 43012
  86.8 14.6 %copy-start.12 = (bf16[3584,64]{0,1:T(8,128)(2,1)S(1)}, bf16[3584,64]{0,1:T(8,128)(2,1)}, u32[]{:S(2)}) copy-start(bf16[3584,64]{0,1:T(8,128)(2,1)} %param.25) | copy-start | bytes 1376260
  86.9 6.6 %collective-permute-start.9 = (bf16[32,3712]{1,0:T(8,128)(2,1)S(1)}, bf16[32,3712]{1,0:T(8,128)(2,1)S(1)}, u32[]{:S(2)}, u32[]{:S(2)}) collective-permute-start(bf16[32,3712]{1,0:T(8,128)(2,1)S(1)} %get-tuple-element.22), channel_id=1, source_target_pairs={{48,0},{0,16},{16,32},{32,48},{49,1},{1,17},{17,33},{33,49},{50,2}... | collective-permute-start | bytes 712712 | tf_op jit(solution)/shard_map/target/ppermute | solution.py:37
  87.3 6.1 %collective-permute-start.10 = (bf16[32,3712]{1,0:T(8,128)(2,1)S(1)}, bf16[32,3712]{1,0:T(8,128)(2,1)S(1)}, u32[]{:S(2)}, u32[]{:S(2)}) collective-permute-start(bf16[32,3712]{1,0:T(8,128)(2,1)S(1)} %get-tuple-element.23), channel_id=1, source_target_pairs={{0,1},{1,0},{2,3},{3,2},{4,5},{5,4},{6,7},{7,6},{8,9},{9,8},{10,11... | collective-permute-start | bytes 712712 | tf_op jit(solution)/shard_map/target/ppermute | solution.py:45
  87.9 5.6 %collective-permute-start.11 = (bf16[32,3712]{1,0:T(8,128)(2,1)S(1)}, bf16[32,3712]{1,0:T(8,128)(2,1)S(1)}, u32[]{:S(2)}, u32[]{:S(2)}) collective-permute-start(bf16[32,3712]{1,0:T(8,128)(2,1)S(1)} %get-tuple-element.24), channel_id=1, source_target_pairs={{16,0},{32,16},{48,32},{0,48},{17,1},{33,17},{49,33},{1,49},{18,2}... | collective-permute-start | bytes 712712 | tf_op jit(solution)/shard_map/target/ppermute | solution.py:37
  94.4 16.9 %all-to-all-start.3 = ((bf16[16,2,3712]{2,1,0:T(2,128)(2,1)}), bf16[16,2,3712]{2,1,0:T(2,128)(2,1)S(1)}, u32[]{:S(2)}, u32[]{:S(2)}) async-start(bf16[16,2,3712]{2,1,0:T(2,128)(2,1)} %target.1), calls=%async_computation.3 | async-start | bytes 475136 | tf_op jit(solution)/shard_map/target/all_to_all | solution.py:282
  141.0 2.8 %collective-permute-start.13 = (bf16[128,128]{1,0:T(8,128)(2,1)S(1)}, bf16[128,128]{1,0:T(8,128)(2,1)S(1)}, u32[]{:S(2)}, u32[]{:S(2)}) collective-permute-start(bf16[128,128]{1,0:T(8,128)(2,1)S(1)} %pad_maximum_fusion.2), channel_id=1, source_target_pairs={{2,0},{4,2},{6,4},{8,6},{10,8},{12,10},{14,12},{0,14},{3,1},{5,3},... | collective-permute-start | bytes 98312 | tf_op jit(solution)/shard_map/columns/ppermute | solution.py:41
  142.2 3.7 %collective-permute-start.12 = (bf16[128,128]{1,0:T(8,128)(2,1)S(1)}, bf16[128,128]{1,0:T(8,128)(2,1)S(1)}, u32[]{:S(2)}, u32[]{:S(2)}) collective-permute-start(bf16[128,128]{1,0:T(8,128)(2,1)S(1)} %pad_maximum_fusion.2), channel_id=1, source_target_pairs={{4,0},{6,2},{8,4},{10,6},{12,8},{14,10},{0,12},{2,14},{5,1},{7,3},... | collective-permute-start | bytes 98312 | tf_op jit(solution)/shard_map/columns/ppermute | solution.py:41
  142.4 4.0 %collective-permute-start.14 = (bf16[128,128]{1,0:T(8,128)(2,1)S(1)}, bf16[128,128]{1,0:T(8,128)(2,1)S(1)}, u32[]{:S(2)}, u32[]{:S(2)}) collective-permute-start(bf16[128,128]{1,0:T(8,128)(2,1)S(1)} %pad_maximum_fusion.2), channel_id=1, source_target_pairs={{14,0},{0,2},{2,4},{4,6},{6,8},{8,10},{10,12},{12,14},{15,1},{1,3}... | collective-permute-start | bytes 98312 | tf_op jit(solution)/shard_map/columns/ppermute | solution.py:41
  147.6 21.6 %all-to-all-start.5 = ((bf16[32,128,128]{2,1,0:T(8,128)(2,1)}), bf16[32,128,128]{2,1,0:T(8,128)(2,1)S(1)}, u32[]{:S(2)}, u32[]{:S(2)}) async-start(bf16[32,128,128]{2,1,0:T(8,128)(2,1)} %broadcast_in_dim.8), calls=%async_computation.5 | async-start | bytes 2097152 | tf_op jit(solution)/shard_map/gradients/all_to_all | solution.py:33
